TPU v7x, 32 devices: a whole 2x2x4 slice. The times are simulated.
32 devices in a mesh: box: 16 (over z, y, core), mc: 2 (over x).
Axes of the slice: x: 2, y: 2, z: 4, core: 2. Of those that a mesh axis runs over, the one named last changes fastest.
Arguments:
- base_operator: float32 [16384, 1024], P('box')
- exterior_values: float32 [12288, 128], P('box'), may hold values from -6 to 6
- wire_label: int32 [16, 1024], P('box'), may hold values from 0 to 63, as said below
- wire_material: int32 [64], replicated, may hold values from 0 to 7
- permittivity: float32 [16], P('mc'), parts along dimension 0, may hold values from 1 to 10
- morton_slot: int32 [16], replicated, may hold values from 0 to 15, each once
Outputs:
- merged_rows: float32 [24576, 1536], P(('mc', 'box')), parts along dimension 0
- interface_values: float32 [8192, 128], P(('mc', 'box')), parts along dimension 0
- exterior_flux: float32 [24576, 128], P(('mc', 'box')), parts along dimension 0
There are 2 independent parts, one for each index of `mc`. A program takes and returns all parts, laid end to end along the dimension named above; an argument that names none is the same for every part. Nothing has to cross between parts.
Inputs may be any that keep to these rules, and one draw needn't show every extreme that they name: `wire_label`: along each box's 4 * 256 boundary nodes the labels come in runs of equal wire, each run a whole number of aligned groups of 2 nodes.
All inputs are finite; a program needn't handle non-finite values.
Results may differ from a plain program's by a relative error of at most 0.00014.
Values sent between devices are 32-bit elements; how exact they have to be, the bound alone decides.
A program may use at most 64 MiB of HBM per device.

v0:
```python
import functools

import jax
import jax.numpy as jnp
from jax import lax
from jax.experimental import pallas as pl
from jax.experimental.pallas import tpu as pltpu
from jax.sharding import PartitionSpec as P

F32 = jnp.float32
HIGHEST = lax.Precision.HIGHEST


def flatten_rows(items, boxes):
    return tuple((item.reshape(boxes, -1) for item in items))


def split(x):
    high = x.astype(jnp.bfloat16)
    low = (x - high.astype(F32)).astype(jnp.bfloat16)
    return high, low


def dot_split(a, b):
    (ah, al), (bh, bl) = a, b
    dot = functools.partial(jnp.dot, preferred_element_type=F32)
    return dot(ah, bh) + (dot(ah, bl) + dot(al, bh))


def dot3(a, b):
    return dot_split(split(a), split(b))


def column_of(row):
    return jnp.broadcast_to(row, (128, row.shape[1])).T


def widen(column, width):
    return jnp.concatenate([column] * (width // 128), axis=1)


def norm(x):
    return jnp.sqrt(jnp.sum(x * x))


def eye(n):
    row = lax.broadcasted_iota(jnp.int32, (n, n), 0)
    col = lax.broadcasted_iota(jnp.int32, (n, n), 1)
    return jnp.where(row == col, 1.0, 0.0).astype(F32)


def direct_inverse(s_ref, x_ref):
    n = s_ref.shape[0]
    x_ref[...] = s_ref[...]
    row_id = lax.broadcasted_iota(jnp.int32, (n, n), 0)
    col_id = lax.broadcasted_iota(jnp.int32, (n, n), 1)

    def step(k, carry):
        x = x_ref[...]
        on_row = row_id == k
        on_col = col_id == k
        row = jnp.sum(jnp.where(on_row, x, 0.0), axis=0, keepdims=True)
        col = jnp.sum(jnp.where(on_col, x, 0.0), axis=1, keepdims=True)
        pivot = jnp.sum(jnp.where(on_row & on_col, x, 0.0))
        scaled = row / pivot
        rest = x - col * scaled
        x = jnp.where(on_row, scaled, jnp.where(on_col, -col / pivot, rest))
        x_ref[...] = jnp.where(on_row & on_col, 1.0 / pivot, x)
        return carry

    lax.fori_loop(0, n, step, 0)


def invert(s_ref, x_ref, r_ref):
    s = s_ref[...]
    n = s.shape[0]
    unit = eye(n)
    alpha = n / jnp.sum(s * s)

    def begin(alpha):
        first = unit - alpha * s
        x_ref[...] = alpha * (unit + first)
        residual = dot3(first, first)
        r_ref[...] = residual
        return norm(residual)

    size = begin(alpha)

    def safe_start(_):
        return begin(1.0 / jnp.max(jnp.sum(jnp.abs(s), axis=0, keepdims=True)))

    size = lax.cond(size < 0.9, lambda size: size, safe_start, size)
    s_parts = split(s)

    def going(state):
        size, count = state
        return (size > 1e-2) & (count < 40)

    def improve(state):
        size, count = state
        x = x_ref[...]
        x = x + dot3(x, r_ref[...])
        x_ref[...] = x
        residual = unit - dot_split(s_parts, split(x))
        r_ref[...] = residual
        return norm(residual), count + 1

    size, _ = lax.while_loop(going, improve, (size, jnp.int32(0)))
    x = x_ref[...]
    x = x + dot3(x, r_ref[...])
    residual = unit - jnp.dot(s, x, precision=HIGHEST, preferred_element_type=F32)
    x_ref[...] = x + dot3(x, residual)
    converged = (size < 1e-2) & (norm(residual) < 1e-3)

    @pl.when(jnp.logical_not(converged))
    def _():
        direct_inverse(s_ref, x_ref)


def solve_kernel(
    rows_ref, face_ref, values_ref, scale_ref, other_ref, product_ref,
    merged_ref, interface_ref, flux_ref,
    high_ref, low_ref, value_high, value_low, s_ref, x_ref, r_ref, column_ref,
):
    face = face_ref.shape[0]
    outer = 3 * face
    step = pl.program_id(0)
    scale = scale_ref[...]

    @pl.when(step == 0)
    def _():
        column_ref[...] = column_of(scale)
        own = face_ref[...] * widen(column_ref[outer:, :], 4 * face) * scale
        other = other_ref[...]
        s = own[:, outer:] + other[:, outer:]
        s = 0.5 * (s + s.T)
        diagonal = jnp.sum(s * eye(face), axis=0, keepdims=True)
        inverse_root = lax.rsqrt(diagonal)
        root_column = column_of(inverse_root)
        s_ref[...] = s * inverse_root * widen(root_column, face)
        invert(s_ref, x_ref, r_ref)
        x = split(x_ref[...])

        def solve(right, at):
            width = right.shape[1]
            weights = widen(root_column, width)
            solved = dot_split(x, split(right * weights)) * weights
            high, low = split(solved)
            high_ref[:, at : at + width] = high
            low_ref[:, at : at + width] = low
            return solved

        solve(own[:, :outer], 0)
        solve(other[:, :outer], outer)
        interface_ref[...] = -solve(product_ref[...], 2 * outer)
        high, low = split(values_ref[...])
        value_high[...] = high
        value_low[...] = low

    block = rows_ref.shape[0]
    column = column_ref[pl.ds(pl.multiple_of(step * block, block), block), :]
    rows = rows_ref[...] * widen(column, 4 * face) * scale
    across = split(rows[:, outer:])

    def through(at, width):
        cut = slice(at, at + width)
        return dot_split(across, (high_ref[:, cut], low_ref[:, cut]))

    merged_ref[:, :outer] = rows[:, :outer] - through(0, outer)
    merged_ref[:, outer:] = -through(outer, outer)
    local = dot_split(split(rows[:, :outer]), (value_high[...], value_low[...]))
    flux_ref[...] = local - through(2 * outer, flux_ref.shape[1])


def pair_solve(operator, values, scale, other_rows, product):
    nodes = operator.shape[1]
    face = nodes // 4
    outer = 3 * face
    count = values.shape[1]
    width = 2 * outer + count
    whole = lambda shape: pl.BlockSpec(shape, lambda i: (0, 0))
    rows = lambda width: pl.BlockSpec((face, width), lambda i: (i, 0))
    return pl.pallas_call(
        solve_kernel,
        grid=(3,),
        in_specs=[
            rows(nodes),
            pl.BlockSpec((face, nodes), lambda i: (3, 0)),
            whole(values.shape),
            whole(scale.shape),
            whole(other_rows.shape),
            whole(product.shape),
        ],
        out_specs=[rows(2 * outer), whole((face, count)), rows(count)],
        out_shape=[
            jax.ShapeDtypeStruct((outer, 2 * outer), F32),
            jax.ShapeDtypeStruct((face, count), F32),
            jax.ShapeDtypeStruct((outer, count), F32),
        ],
        scratch_shapes=[
            pltpu.VMEM((face, width), jnp.bfloat16),
            pltpu.VMEM((face, width), jnp.bfloat16),
            pltpu.VMEM((outer, count), jnp.bfloat16),
            pltpu.VMEM((outer, count), jnp.bfloat16),
            pltpu.VMEM((face, face), F32),
            pltpu.VMEM((face, face), F32),
            pltpu.VMEM((face, face), F32),
            pltpu.VMEM((nodes, 128), F32),
        ],
        compiler_params=pltpu.CompilerParams(vmem_limit_bytes=44 * 2**20),
        name="pair_solve",
    )(operator, operator, values, scale, other_rows, product)


def per_device(
    base_operator, exterior_values, wire_label, wire_material, permittivity, morton_slot
):
    highest = lax.Precision.HIGHEST
    boxes = lax.axis_size("box")
    face = base_operator.shape[1] // 4
    outer = 3 * face
    levels = permittivity.shape[0]
    wires = wire_material.shape[0]
    level_match = wire_material[:, None] == jnp.arange(levels, dtype=jnp.int32)[None, :]
    wire_eps = jnp.sum(jnp.where(level_match, permittivity[None, :], 0.0), axis=1)
    wire_match = wire_label[0][:, None] == jnp.arange(wires, dtype=jnp.int32)[None, :]
    node_scale = jnp.sqrt(jnp.sum(jnp.where(wire_match, wire_eps[None, :], 0.0), axis=1))
    rows = base_operator[outer:, :] * node_scale[outer:, None] * node_scale[None, :]
    positions = jnp.arange(boxes, dtype=jnp.int32)
    slot_match = morton_slot[None, :] == positions[:, None]
    inverse = jnp.sum(jnp.where(slot_match, positions[None, :], 0), axis=1)
    partner = jnp.take(inverse, jnp.bitwise_xor(morton_slot, 1), axis=0)
    product = jnp.dot(rows[:, :outer], exterior_values, precision=highest)
    pieces = lax.all_to_all(
        flatten_rows((rows, product), boxes), "box", split_axis=0, concat_axis=0, tiled=True
    )
    moved = tuple((jnp.take(piece, partner, axis=0) for piece in pieces))
    back = lax.all_to_all(moved, "box", split_axis=0, concat_axis=0, tiled=True)
    other_rows = back[0].reshape(rows.shape)
    other_product = back[1].reshape(product.shape)
    return tuple(
        pair_solve(
            base_operator, exterior_values, node_scale[None, :], other_rows,
            product + other_product,
        )
    )


def solution(mesh):
    return jax.shard_map(
        per_device,
        mesh=mesh,
        in_specs=(P("box", None), P("box", None), P("box", None), P(), P("mc"), P()),
        out_specs=(P(("mc", "box"), None), P(("mc", "box"), None), P(("mc", "box"), None)),
        check_vma=False,
    )
```

profile of v0, /device:TPU:0, one launch (start us, length us, event | category | flops | bytes accessed | tf_op | source)
XLA Modules:
  0.0 103.0 jit_solution(949586358308461469)
XLA Ops:
  0.6 0.0 copy-start.2
  0.6 0.8 select_reduce_fusion.2
  1.4 0.8 select_reduce_fusion
  2.2 1.4 %multiply_multiply_fusion = f32[256,1024]{1,0:T(8,128)S(1)} fusion(f32[1024,1024]{1,0:T(8,128)} %face_ref.1, f32[1024]{0:T(1024)S(1)} %sqrt.14, f32[256]{0:T(256)S(1)} %slice.10), kind=kLoop, calls=%fused_computation.5 | loop fusion | flops 524288 | bytes 2102272 | tf_op jit(solution)/shard_map/mul | solution.py:228
  3.6 2.4 %fusion = f32[256,128]{1,0:T(8,128)} fusion(f32[768,128]{1,0:T(8,128)} %values_ref.1, f32[256,1024]{1,0:T(8,128)S(1)} %multiply_multiply_fusion), kind=kOutput, calls=%fused_computation.6 | convolution fusion | flops 301989888 | bytes 1310720 | tf_op jit(solution)/shard_map/dot_general | solution.py:233
  6.0 7.4 %all-to-all-start.2 = ((f32[16,1,2048]{2,1,0:T(1,128)}), f32[16,1,2048]{2,1,0:T(1,128)S(1)}, u32[]{:S(2)}, u32[]{:S(2)}) async-start(f32[16,1,2048]{2,1,0:T(1,128)} %bitcast.3), calls=%async_computation.2 | async-start | bytes 262144 | tf_op jit(solution)/shard_map/all_to_all | solution.py:234
  13.4 2.2 %all_to_all.24 = f32[16,1,16384]{2,1,0:T(1,128)} reshape(f32[256,1024]{1,0:T(8,128)S(1)} %multiply_multiply_fusion) | data formatting | bytes 2097152 | tf_op jit(solution)/shard_map/all_to_all | solution.py:234
  15.7 5.7 %all-to-all-done.2 = f32[16,1,2048]{2,1,0:T(1,128)S(1)} async-done(((f32[16,1,2048]{2,1,0:T(1,128)}), f32[16,1,2048]{2,1,0:T(1,128)S(1)}, u32[]{:S(2)}, u32[]{:S(2)}) %all-to-all-start.2) | async-done | bytes 131104 | tf_op jit(solution)/shard_map/all_to_all | solution.py:234
  21.4 3.7 %all-to-all-start = ((f32[16,1,16384]{2,1,0:T(1,128)}), f32[16,1,16384]{2,1,0:T(1,128)S(1)}, u32[]{:S(2)}, u32[]{:S(2)}) async-start(f32[16,1,16384]{2,1,0:T(1,128)} %all_to_all.24), calls=%async_computation | async-start | bytes 2097152 | tf_op jit(solution)/shard_map/all_to_all | solution.py:234
  25.0 0.0 copy-done.2
  25.1 0.1 select_reduce_fusion.1
  25.2 0.7 gather_fusion
  25.9 0.6 gather_fusion.2
  26.5 0.1 bitcast_select_fusion.1
  26.6 0.8 copy.14
  27.4 20.5 %all-to-all-done = f32[16,1,16384]{2,1,0:T(1,128)S(1)} async-done(((f32[16,1,16384]{2,1,0:T(1,128)}), f32[16,1,16384]{2,1,0:T(1,128)S(1)}, u32[]{:S(2)}, u32[]{:S(2)}) %all-to-all-start) | async-done | bytes 1048608 | tf_op jit(solution)/shard_map/all_to_all | solution.py:234
  47.9 6.8 %all-to-all-start.3 = ((f32[16,1,2048]{2,1,0:T(1,128)}), f32[16,1,2048]{2,1,0:T(1,128)S(1)}, u32[]{:S(2)}, u32[]{:S(2)}) async-start(f32[16,1,2048]{2,1,0:T(1,128)} %copy.14), calls=%async_computation.3 | async-start | bytes 262144 | tf_op jit(solution)/shard_map/all_to_all | solution.py:238
  54.8 0.6 copy.19
  55.4 0.9 gather_fusion.1
  56.3 0.1 bitcast_select_fusion
  56.4 0.0 copy-start.1
  56.4 2.0 %copy.12 = f32[16,1,16384]{2,1,0:T(1,128)} copy(f32[16,1,16384]{2,0,1:T(8,128)S(1)} %bitcast_select_fusion) | data formatting | bytes 2097152 | tf_op jit(solution)/shard_map/jit(_take)/select_n | solution.py:237
  58.5 4.2 %all-to-all-done.3 = f32[16,1,2048]{2,1,0:T(1,128)S(1)} async-done(((f32[16,1,2048]{2,1,0:T(1,128)}), f32[16,1,2048]{2,1,0:T(1,128)S(1)}, u32[]{:S(2)}, u32[]{:S(2)}) %all-to-all-start.3) | async-done | bytes 131104 | tf_op jit(solution)/shard_map/all_to_all | solution.py:238
  62.7 3.8 %all-to-all-start.1 = ((f32[16,1,16384]{2,1,0:T(1,128)}), f32[16,1,16384]{2,1,0:T(1,128)S(1)}, u32[]{:S(2)}, u32[]{:S(2)}) async-start(f32[16,1,16384]{2,1,0:T(1,128)} %copy.12), calls=%async_computation.1 | async-start | bytes 2097152 | tf_op jit(solution)/shard_map/all_to_all | solution.py:238
  66.5 0.9 add.19.product_ref
  67.5 21.8 %all-to-all-done.1 = f32[16,1,16384]{2,1,0:T(1,128)S(1)} async-done(((f32[16,1,16384]{2,1,0:T(1,128)}), f32[16,1,16384]{2,1,0:T(1,128)S(1)}, u32[]{:S(2)}, u32[]{:S(2)}) %all-to-all-start.1) | async-done | bytes 1048608 | tf_op jit(solution)/shard_map/all_to_all | solution.py:238
  89.3 2.6 %reduce = f32[16,16384]{1,0:T(8,128)S(1)} reduce(f32[16,1,16384]{2,1,0:T(1,128)S(1)} %all-to-all-done.1, f32[]{:T(128)} %constant.47), dimensions={1}, to_apply=%all_to_all.27.reduce_sub_computation | reduce | bytes 2097156 | tf_op jit(solution)/shard_map/all_to_all | solution.py:238
  91.9 0.2 reshape.100.other_ref
  92.1 0.0 copy-done.1
  92.1 0.0 copy-start
  92.1 2.2 %copy-done = f32[1024,1024]{1,0:T(8,128)S(1)} copy-done((f32[1024,1024]{1,0:T(8,128)S(1)}, f32[1024,1024]{1,0:T(8,128)}, u32[]{:S(2)}) %copy-start) | copy-done | bytes 4194328
  94.3 8.8 %pair_solve.1 = (f32[768,1536]{1,0:T(8,128)}, f32[256,128]{1,0:T(8,128)}, f32[768,128]{1,0:T(8,128)}) custom-call(f32[1024,1024]{1,0:T(8,128)S(1)} %copy-done, f32[1024,1024]{1,0:T(8,128)S(1)} %copy-done, f32[768,128]{1,0:T(8,128)S(1)} %copy-done.1, f32[1,1024]{1,0:T(1,128)S(1)} %bitcast.15, f32[256,1024]{1,0:T(8,128)S(1)} %reshape.100.other_ref, ...), custom_call_target="tpu_custom_call" | custom-call | tf_op jit(solution)/shard_map/pair_solve/pallas_call | solution.py:183
  (7 shorter events, 0.1 us)
Async XLA Ops:
  0.6 24.4 %copy-start.2 = (s32[16]{0:T(128)S(1)}, s32[16]{0:T(128)}, u32[]{:S(2)}) copy-start(s32[16]{0:T(128)} %param.11) | copy-start | bytes 196
  6.0 15.3 %all-to-all-start.2 = ((f32[16,1,2048]{2,1,0:T(1,128)}), f32[16,1,2048]{2,1,0:T(1,128)S(1)}, u32[]{:S(2)}, u32[]{:S(2)}) async-start(f32[16,1,2048]{2,1,0:T(1,128)} %bitcast.3), calls=%async_computation.2 | async-start | bytes 262144 | tf_op jit(solution)/shard_map/all_to_all | solution.py:234
  21.4 26.6 %all-to-all-start = ((f32[16,1,16384]{2,1,0:T(1,128)}), f32[16,1,16384]{2,1,0:T(1,128)S(1)}, u32[]{:S(2)}, u32[]{:S(2)}) async-start(f32[16,1,16384]{2,1,0:T(1,128)} %all_to_all.24), calls=%async_computation | async-start | bytes 2097152 | tf_op jit(solution)/shard_map/all_to_all | solution.py:234
  47.9 14.8 %all-to-all-start.3 = ((f32[16,1,2048]{2,1,0:T(1,128)}), f32[16,1,2048]{2,1,0:T(1,128)S(1)}, u32[]{:S(2)}, u32[]{:S(2)}) async-start(f32[16,1,2048]{2,1,0:T(1,128)} %copy.14), calls=%async_computation.3 | async-start | bytes 262144 | tf_op jit(solution)/shard_map/all_to_all | solution.py:238
  56.4 35.6 %copy-start.1 = (f32[768,128]{1,0:T(8,128)S(1)}, f32[768,128]{1,0:T(8,128)}, u32[]{:S(2)}) copy-start(f32[768,128]{1,0:T(8,128)} %values_ref.1) | copy-start | bytes 1179652
  62.7 26.6 %all-to-all-start.1 = ((f32[16,1,16384]{2,1,0:T(1,128)}), f32[16,1,16384]{2,1,0:T(1,128)S(1)}, u32[]{:S(2)}, u32[]{:S(2)}) async-start(f32[16,1,16384]{2,1,0:T(1,128)} %copy.12), calls=%async_computation.1 | async-start | bytes 2097152 | tf_op jit(solution)/shard_map/all_to_all | solution.py:238
  92.1 2.2 %copy-start = (f32[1024,1024]{1,0:T(8,128)S(1)}, f32[1024,1024]{1,0:T(8,128)}, u32[]{:S(2)}) copy-start(f32[1024,1024]{1,0:T(8,128)} %face_ref.1) | copy-start | bytes 12582916
where the time goes:
time: 105 us; the launch traced here: 103 us
  waiting for transfers between devices  52.2 us (50%)
  starting transfers between devices  21.7 us (21%)
  local copies, waits for them, and re-layouts  10.3 us (10%)
  Pallas kernels  8.77 us (8%)
  other arithmetic  6.83 us (7%)
  matrix products  2.44 us (2%)
    all_to_all x2, waiting for transfers between devices, per_device(): lax.all_to_all(flatten_rows((rows, product), boxes), 'box', split_axis=0,...  26.2 us
    all_to_all x2, waiting for transfers between devices, per_device(): back = lax.all_to_all(moved, 'box', split_axis=0, concat_axis=0, tiled=True)  26 us
    all_to_all x2, starting transfers between devices, per_device(): lax.all_to_all(flatten_rows((rows, product), boxes), 'box', split_axis=0,...  11 us
    all_to_all x2, starting transfers between devices, per_device(): back = lax.all_to_all(moved, 'box', split_axis=0, concat_axis=0, tiled=True)  10.7 us
    pallas_call x1, Pallas kernels, pair_solve(): pl.pallas_call(solve_kernel, grid=(3,), in_specs=[rows(nodes), pl.BlockSp...  8.77 us
    unnamed x8, local copies, waits for them, and re-layouts  2.85 us
    select_n x2, local copies, waits for them, and re-layouts, per_device(): moved = tuple((jnp.take(piece, partner, axis=0) for piece in pieces))  2.84 us
    all_to_all x1, other arithmetic, per_device(): back = lax.all_to_all(moved, 'box', split_axis=0, concat_axis=0, tiled=True)  2.61 us
  transfers between devices with their start and end apart: 4, of which 4 were waited for; matrix products, arithmetic and copies ran while one was open for 7% of the time, Pallas kernels for 0%

commit v1 on v0

--- a/solution.py
+++ b/solution.py
@@ -9,10 +9,6 @@
 
 F32 = jnp.float32
 HIGHEST = lax.Precision.HIGHEST
-
-
-def flatten_rows(items, boxes):
-    return tuple((item.reshape(boxes, -1) for item in items))
 
 
 def split(x):
@@ -212,38 +208,232 @@
     )(operator, operator, values, scale, other_rows, product)
 
 
+def exchange_kernel(
+    boxes, samples,
+    face_ref, values_ref, label_ref, material_ref, permittivity_ref, slot_ref,
+    other_ref, total_ref, scale_ref,
+    message, gathered, staged, final, partner,
+    send_first, receive_first, send_second, receive_second, send_third, receive_third,
+):
+    me = lax.axis_index("box")
+    sample = lax.axis_index("mc")
+    face, nodes = face_ref.shape
+    outer = 3 * face
+    share = face // samples
+    across = max(1, boxes * 8 // share)
+    width = nodes // across
+    height = share * across // boxes
+    tiles = width // 128
+    part = height * tiles
+    strip = face // boxes
+    shift = lambda k: lax.rem(me + k + boxes, boxes)
+    target = lambda box: {"box": box, "mc": sample}
+
+    barrier = pltpu.get_barrier_semaphore()
+
+    def greet(k, carry):
+        pl.semaphore_signal(
+            barrier, inc=1, device_id=target(shift(k)), device_id_type=pl.DeviceIdType.MESH
+        )
+        return carry
+
+    lax.fori_loop(1, boxes, greet, 0)
+    twins = [lax.rem(sample + t, samples) for t in range(1, samples)]
+    for twin in twins:
+        pl.semaphore_signal(
+            barrier, inc=1, device_id={"box": me, "mc": twin},
+            device_id_type=pl.DeviceIdType.MESH,
+        )
+
+    def place(j):
+        row = (j // across) * height
+        column = lax.rem(j, across) * width
+        return row, column
+
+    def fill(j, carry):
+        row, column = place(j)
+        for t in range(tiles):
+            message[j, t * height : (t + 1) * height, :] = face_ref[
+                pl.ds(pl.multiple_of(sample * share + row, 8), height),
+                pl.ds(pl.multiple_of(column + 128 * t, 128), 128),
+            ]
+        return carry
+
+    lax.fori_loop(0, boxes, fill, 0)
+
+    label = label_ref[...]
+    level = jnp.zeros_like(label)
+    for w in range(material_ref.shape[0]):
+        level = jnp.where(label == w, material_ref[w], level)
+    eps = jnp.zeros(label.shape, F32)
+    for l in range(permittivity_ref.shape[0]):
+        eps = jnp.where(level == l, permittivity_ref[l], eps)
+    root = jnp.sqrt(eps)
+    as_row = lambda x: jnp.concatenate([x[t : t + 1, :] for t in range(x.shape[0])], axis=1)
+    scale = as_row(root)
+    scale_ref[...] = scale
+    column = column_of(scale[:, outer:])
+    own = face_ref[:, :outer] * widen(column, outer) * scale[:, :outer]
+    product = dot3(own, values_ref[...])
+    total_ref[...] = product
+    for j in range(boxes):
+        message[j, part : part + strip, :] = product[j * strip : (j + 1) * strip, :]
+    tail = message.shape[1] - root.shape[0]
+    message[:, tail:, :] = jnp.broadcast_to(root[None], (boxes,) + root.shape)
+
+    pl.semaphore_wait(barrier, boxes - 1 + samples - 1)
+
+    def first(k, carry):
+        box = shift(k)
+        pltpu.make_async_remote_copy(
+            src_ref=message.at[box], dst_ref=gathered.at[me],
+            send_sem=send_first, recv_sem=receive_first,
+            device_id=target(box), device_id_type=pl.DeviceIdType.MESH,
+        ).start()
+        return carry
+
+    lax.fori_loop(1, boxes, first, 0)
+    gathered[me] = message[me]
+
+    def find(p, carry):
+        wanted = slot_ref[p] ^ 1
+        partner[p] = lax.fori_loop(
+            0, boxes, lambda i, at: jnp.where(slot_ref[i] == wanted, i, at), jnp.int32(0)
+        )
+        return carry
+
+    lax.fori_loop(0, boxes, find, 0)
+
+    def drain(buffer, semaphore):
+        pltpu.make_async_copy(buffer, buffer, semaphore).wait()
+
+    drain(gathered.at[pl.ds(0, boxes - 1)], receive_first)
+
+    kept = staged.shape[1]
+
+    def stage(p, carry):
+        staged[p] = gathered[partner[p], 0:kept, :]
+        return carry
+
+    lax.fori_loop(0, boxes, stage, 0)
+
+    def second(k, carry):
+        box = shift(k)
+        pltpu.make_async_remote_copy(
+            src_ref=staged.at[box], dst_ref=final.at[sample, me],
+            send_sem=send_second, recv_sem=receive_second.at[k],
+            device_id=target(box), device_id_type=pl.DeviceIdType.MESH,
+        ).start()
+        return carry
+
+    lax.fori_loop(1, boxes, second, 0)
+    final[sample, me] = staged[me]
+
+    def forward(source):
+        for t, twin in enumerate(twins):
+            block = final.at[sample, source, pl.ds(0, part)]
+            pltpu.make_async_remote_copy(
+                src_ref=block, dst_ref=block,
+                send_sem=send_third.at[t], recv_sem=receive_third.at[t],
+                device_id={"box": me, "mc": twin}, device_id_type=pl.DeviceIdType.MESH,
+            ).start()
+
+    forward(me)
+
+    def third(k, carry):
+        source = shift(-k)
+        drain(final.at[sample, source], receive_second.at[k])
+        forward(source)
+        return carry
+
+    lax.fori_loop(1, boxes, third, 0)
+
+    partner_scale = as_row(gathered[partner[me], tail:, :])
+    partner_column = column_of(partner_scale[:, outer:])
+
+    def collect(group):
+        def body(j, carry):
+            row, column = place(j)
+            for t in range(tiles):
+                other_ref[
+                    pl.ds(pl.multiple_of(group * share + row, 8), height),
+                    pl.ds(pl.multiple_of(column + 128 * t, 128), 128),
+                ] = final[group, j, t * height : (t + 1) * height, :]
+            return carry
+
+        lax.fori_loop(0, boxes, body, 0)
+
+    collect(sample)
+    for j in range(boxes):
+        total_ref[j * strip : (j + 1) * strip, :] += final[sample, j, part : part + strip, :]
+    for t, twin in enumerate(twins):
+        origin = lax.rem(sample + samples - (t + 1), samples)
+        drain(final.at[origin, :, pl.ds(0, part)], receive_third.at[t])
+        collect(origin)
+    other_ref[...] = other_ref[...] * widen(partner_column, nodes) * partner_scale
+
+    drain(message.at[pl.ds(0, boxes - 1)], send_first)
+    drain(staged.at[pl.ds(0, boxes - 1)], send_second)
+    for t in range(samples - 1):
+        drain(final.at[sample, :, pl.ds(0, part)], send_third.at[t])
+
+
+def exchange(operator, values, label, material, permittivity, slot):
+    boxes = lax.axis_size("box")
+    samples = lax.axis_size("mc")
+    nodes = operator.shape[1]
+    face = nodes // 4
+    count = values.shape[1]
+    label = label.reshape(nodes // 128, 128)
+    part = face // samples * nodes // boxes // 128
+    strip = -(-face // boxes // 8) * 8
+    kept = part + strip
+    whole = lambda shape: pl.BlockSpec(shape, lambda i: (0, 0))
+    scalars = pl.BlockSpec(memory_space=pltpu.SMEM)
+    return pl.pallas_call(
+        functools.partial(exchange_kernel, boxes, samples),
+        grid=(1,),
+        in_specs=[
+            pl.BlockSpec((face, nodes), lambda i: (3, 0)),
+            whole(values.shape),
+            whole(label.shape),
+            scalars,
+            scalars,
+            scalars,
+        ],
+        out_specs=[whole((face, nodes)), whole((face, count)), whole((1, nodes))],
+        out_shape=[
+            jax.ShapeDtypeStruct((face, nodes), F32),
+            jax.ShapeDtypeStruct((face, count), F32),
+            jax.ShapeDtypeStruct((1, nodes), F32),
+        ],
+        scratch_shapes=[
+            pltpu.VMEM((boxes, kept + nodes // 128, 128), F32),
+            pltpu.VMEM((boxes, kept + nodes // 128, 128), F32),
+            pltpu.VMEM((boxes, kept, 128), F32),
+            pltpu.VMEM((samples, boxes, kept, 128), F32),
+            pltpu.SMEM((boxes,), jnp.int32),
+            pltpu.SemaphoreType.DMA,
+            pltpu.SemaphoreType.DMA,
+            pltpu.SemaphoreType.DMA,
+            pltpu.SemaphoreType.DMA((boxes,)),
+            pltpu.SemaphoreType.DMA((max(1, samples - 1),)),
+            pltpu.SemaphoreType.DMA((max(1, samples - 1),)),
+        ],
+        compiler_params=pltpu.CompilerParams(
+            collective_id=0, has_side_effects=True, vmem_limit_bytes=32 * 2**20
+        ),
+        name="exchange",
+    )(operator, values, label, material, permittivity, slot)
+
+
 def per_device(
     base_operator, exterior_values, wire_label, wire_material, permittivity, morton_slot
 ):
-    highest = lax.Precision.HIGHEST
-    boxes = lax.axis_size("box")
-    face = base_operator.shape[1] // 4
-    outer = 3 * face
-    levels = permittivity.shape[0]
-    wires = wire_material.shape[0]
-    level_match = wire_material[:, None] == jnp.arange(levels, dtype=jnp.int32)[None, :]
-    wire_eps = jnp.sum(jnp.where(level_match, permittivity[None, :], 0.0), axis=1)
-    wire_match = wire_label[0][:, None] == jnp.arange(wires, dtype=jnp.int32)[None, :]
-    node_scale = jnp.sqrt(jnp.sum(jnp.where(wire_match, wire_eps[None, :], 0.0), axis=1))
-    rows = base_operator[outer:, :] * node_scale[outer:, None] * node_scale[None, :]
-    positions = jnp.arange(boxes, dtype=jnp.int32)
-    slot_match = morton_slot[None, :] == positions[:, None]
-    inverse = jnp.sum(jnp.where(slot_match, positions[None, :], 0), axis=1)
-    partner = jnp.take(inverse, jnp.bitwise_xor(morton_slot, 1), axis=0)
-    product = jnp.dot(rows[:, :outer], exterior_values, precision=highest)
-    pieces = lax.all_to_all(
-        flatten_rows((rows, product), boxes), "box", split_axis=0, concat_axis=0, tiled=True
+    other_rows, product, scale = exchange(
+        base_operator, exterior_values, wire_label, wire_material, permittivity, morton_slot
     )
-    moved = tuple((jnp.take(piece, partner, axis=0) for piece in pieces))
-    back = lax.all_to_all(moved, "box", split_axis=0, concat_axis=0, tiled=True)
-    other_rows = back[0].reshape(rows.shape)
-    other_product = back[1].reshape(product.shape)
-    return tuple(
-        pair_solve(
-            base_operator, exterior_values, node_scale[None, :], other_rows,
-            product + other_product,
-        )
-    )
+    return tuple(pair_solve(base_operator, exterior_values, scale, other_rows, product))
 
 
 def solution(mesh):

time: 105 us -> 61.8 us (0.59)
  the two profiles are of different devices: /device:TPU:0 before, /device:TPU:24 now
where the time goes in v1:
time: 61.8 us; the launch traced here: 61.6 us
  Pallas kernels  55.1 us (89%)
  local copies, waits for them, and re-layouts  5.83 us (9%)
  between operations  0.67 us (1%)
    pallas_call x1, Pallas kernels, exchange(): pl.pallas_call(functools.partial(exchange_kernel, boxes, samples), grid=(...  46.4 us
    pallas_call x1, Pallas kernels, pair_solve(): pl.pallas_call(solve_kernel, grid=(3,), in_specs=[rows(nodes), pl.BlockSp...  8.67 us
    unnamed x16, local copies, waits for them, and re-layouts  5.83 us

profile of v1, /device:TPU:24, one launch (start us, length us, event | category | flops | bytes accessed | tf_op | source)
XLA Modules:
  0.0 61.6 jit_solution(7816532558077334125)
XLA Ops:
  0.6 0.0 copy-start
  0.6 2.2 %copy-done = f32[1024,1024]{1,0:T(8,128)S(1)} copy-done((f32[1024,1024]{1,0:T(8,128)S(1)}, f32[1024,1024]{1,0:T(8,128)}, u32[]{:S(2)}) %copy-start) | copy-done | bytes 4194328
  2.8 0.0 copy-start.2
  2.8 1.0 %copy-done.2 = f32[768,128]{1,0:T(8,128)S(1)} copy-done((f32[768,128]{1,0:T(8,128)S(1)}, f32[768,128]{1,0:T(8,128)}, u32[]{:S(2)}) %copy-start.2) | copy-done | bytes 393240
  3.8 0.0 copy-start.4
  3.8 0.7 %copy-done.4 = s32[1,1024]{1,0:T(1,128)S(1)} copy-done((s32[1,1024]{1,0:T(1,128)S(1)}, s32[1,1024]{1,0:T(1,128)}, u32[]{:S(2)}) %copy-start.4) | copy-done | bytes 4120
  4.5 0.0 copy-start.5
  4.5 0.7 %copy-done.5 = s32[64]{0:T(128)S(1)} copy-done((s32[64]{0:T(128)S(1)}, s32[64]{0:T(128)}, u32[]{:S(2)}) %copy-start.5) | copy-done | bytes 280
  5.2 0.0 copy-start.6
  5.2 0.7 %copy-done.6 = f32[8]{0:T(128)S(1)} copy-done((f32[8]{0:T(128)S(1)}, f32[8]{0:T(128)}, u32[]{:S(2)}) %copy-start.6) | copy-done | bytes 56
  5.8 0.0 copy-start.7
  5.8 0.7 %copy-done.7 = s32[16]{0:T(128)S(1)} copy-done((s32[16]{0:T(128)S(1)}, s32[16]{0:T(128)}, u32[]{:S(2)}) %copy-start.7) | copy-done | bytes 88
  6.5 0.0 copy-start.1
  6.5 0.0 copy-start.3
  6.5 46.4 %exchange.1 = (f32[256,1024]{1,0:T(8,128)S(1)}, f32[256,128]{1,0:T(8,128)S(1)}, f32[1,1024]{1,0:T(1,128)S(1)}) custom-call(f32[1024,1024]{1,0:T(8,128)S(1)} %copy-done, f32[768,128]{1,0:T(8,128)S(1)} %copy-done.2, s32[8,128]{1,0:T(8,128)S(1)} %bitcast.1, s32[64]{0:T(128)S(1)} %copy-done.5, f32[8]{0:T(128)S(1)} %copy-done.6, s32[16]{0:T(128)S(1)} %copy-done.7), custom_call_target="tpu_custom_call" | custom-call | tf_op jit(solution)/shard_map/exchange/pallas_call | solution.py:393
  52.9 0.0 copy-done.1
  52.9 0.0 copy-done.3
  52.9 8.7 %pair_solve.1 = (f32[768,1536]{1,0:T(8,128)}, f32[256,128]{1,0:T(8,128)}, f32[768,128]{1,0:T(8,128)}) custom-call(f32[1024,1024]{1,0:T(8,128)S(1)} %copy-done.1, f32[1024,1024]{1,0:T(8,128)S(1)} %copy-done.1, f32[768,128]{1,0:T(8,128)S(1)} %copy-done.3, f32[1,1024]{1,0:T(1,128)S(1)} %get-tuple-element.6.scale_ref, ...), custom_call_target="tpu_custom_call" | custom-call | tf_op jit(solution)/shard_map/pair_solve/pallas_call | solution.py:179
Async XLA Ops:
  0.6 2.2 %copy-start = (f32[1024,1024]{1,0:T(8,128)S(1)}, f32[1024,1024]{1,0:T(8,128)}, u32[]{:S(2)}) copy-start(f32[1024,1024]{1,0:T(8,128)} %face_ref.3) | copy-start | bytes 12582916
  2.8 1.0 %copy-start.2 = (f32[768,128]{1,0:T(8,128)S(1)}, f32[768,128]{1,0:T(8,128)}, u32[]{:S(2)}) copy-start(f32[768,128]{1,0:T(8,128)} %values_ref.3) | copy-start | bytes 1179652
  3.8 0.7 %copy-start.4 = (s32[1,1024]{1,0:T(1,128)S(1)}, s32[1,1024]{1,0:T(1,128)}, u32[]{:S(2)}) copy-start(s32[1,1024]{1,0:T(1,128)} %param.8) | copy-start | bytes 12292
  4.5 0.7 %copy-start.5 = (s32[64]{0:T(128)S(1)}, s32[64]{0:T(128)}, u32[]{:S(2)}) copy-start(s32[64]{0:T(128)} %material_ref.1) | copy-start | bytes 772
  5.2 0.7 %copy-start.6 = (f32[8]{0:T(128)S(1)}, f32[8]{0:T(128)}, u32[]{:S(2)}) copy-start(f32[8]{0:T(128)} %permittivity_ref.1) | copy-start | bytes 100
  5.8 0.7 %copy-start.7 = (s32[16]{0:T(128)S(1)}, s32[16]{0:T(128)}, u32[]{:S(2)}) copy-start(s32[16]{0:T(128)} %slot_ref.1) | copy-start | bytes 196
  6.5 46.4 %copy-start.1 = (f32[1024,1024]{1,0:T(8,128)S(1)}, f32[1024,1024]{1,0:T(8,128)}, u32[]{:S(2)}) copy-start(f32[1024,1024]{1,0:T(8,128)} %face_ref.3) | copy-start | bytes 12582916
  6.5 46.4 %copy-start.3 = (f32[768,128]{1,0:T(8,128)S(1)}, f32[768,128]{1,0:T(8,128)}, u32[]{:S(2)}) copy-start(f32[768,128]{1,0:T(8,128)} %values_ref.3) | copy-start | bytes 1179652

commit v2 on v1

v2 whole, which is shorter than its diff:
```python
import functools

import jax
import jax.numpy as jnp
from jax import lax
from jax.experimental import pallas as pl
from jax.experimental.pallas import tpu as pltpu
from jax.sharding import PartitionSpec as P

F32 = jnp.float32
HIGHEST = lax.Precision.HIGHEST


def split(x):
    high = x.astype(jnp.bfloat16)
    low = (x - high.astype(F32)).astype(jnp.bfloat16)
    return high, low


def dot_split(a, b):
    (ah, al), (bh, bl) = a, b
    dot = functools.partial(jnp.dot, preferred_element_type=F32)
    return dot(ah, bh) + (dot(ah, bl) + dot(al, bh))


def dot3(a, b):
    return dot_split(split(a), split(b))


def column_of(row):
    return jnp.broadcast_to(row, (128, row.shape[1])).T


def widen(column, width):
    return jnp.concatenate([column] * (width // 128), axis=1)


def norm(x):
    return jnp.sqrt(jnp.sum(x * x))


def eye(n):
    row = lax.broadcasted_iota(jnp.int32, (n, n), 0)
    col = lax.broadcasted_iota(jnp.int32, (n, n), 1)
    return jnp.where(row == col, 1.0, 0.0).astype(F32)


def direct_inverse(s_ref, x_ref):
    n = s_ref.shape[0]
    x_ref[...] = s_ref[...]
    row_id = lax.broadcasted_iota(jnp.int32, (n, n), 0)
    col_id = lax.broadcasted_iota(jnp.int32, (n, n), 1)

    def step(k, carry):
        x = x_ref[...]
        on_row = row_id == k
        on_col = col_id == k
        row = jnp.sum(jnp.where(on_row, x, 0.0), axis=0, keepdims=True)
        col = jnp.sum(jnp.where(on_col, x, 0.0), axis=1, keepdims=True)
        pivot = jnp.sum(jnp.where(on_row & on_col, x, 0.0))
        scaled = row / pivot
        rest = x - col * scaled
        x = jnp.where(on_row, scaled, jnp.where(on_col, -col / pivot, rest))
        x_ref[...] = jnp.where(on_row & on_col, 1.0 / pivot, x)
        return carry

    lax.fori_loop(0, n, step, 0)


def invert(s_ref, x_ref, r_ref):
    s = s_ref[...]
    n = s.shape[0]
    unit = eye(n)
    alpha = n / jnp.sum(s * s)

    def begin(alpha):
        first = unit - alpha * s
        x_ref[...] = alpha * (unit + first)
        residual = dot3(first, first)
        r_ref[...] = residual
        return norm(residual)

    size = begin(alpha)

    def safe_start(_):
        return begin(1.0 / jnp.max(jnp.sum(jnp.abs(s), axis=0, keepdims=True)))

    size = lax.cond(size < 0.9, lambda size: size, safe_start, size)
    s_parts = split(s)

    def going(state):
        size, count = state
        return (size > 1e-2) & (count < 40)

    def improve(state):
        size, count = state
        x = x_ref[...]
        x = x + dot3(x, r_ref[...])
        x_ref[...] = x
        residual = unit - dot_split(s_parts, split(x))
        r_ref[...] = residual
        return norm(residual), count + 1

    size, _ = lax.while_loop(going, improve, (size, jnp.int32(0)))
    x = x_ref[...]
    x = x + dot3(x, r_ref[...])
    residual = unit - jnp.dot(s, x, precision=HIGHEST, preferred_element_type=F32)
    x_ref[...] = x + dot3(x, residual)
    converged = (size < 1e-2) & (norm(residual) < 1e-3)

    @pl.when(jnp.logical_not(converged))
    def _():
        direct_inverse(s_ref, x_ref)


def solve_kernel(
    rows_ref, face_ref, values_ref, scale_ref, schur_ref, other_ref, product_ref,
    merged_ref, interface_ref, flux_ref,
    high_ref, low_ref, value_high, value_low, s_ref, x_ref, r_ref, column_ref,
):
    face = face_ref.shape[0]
    outer = 3 * face
    step = pl.program_id(0)
    scale = scale_ref[...]

    @pl.when(step == 0)
    def _():
        column_ref[...] = column_of(scale)
        own = face_ref[...] * widen(column_ref[outer:, :], 4 * face) * scale
        s = schur_ref[...]
        diagonal = jnp.sum(s * eye(face), axis=0, keepdims=True)
        inverse_root = lax.rsqrt(diagonal)
        root_column = column_of(inverse_root)
        s_ref[...] = s * inverse_root * widen(root_column, face)
        invert(s_ref, x_ref, r_ref)
        x = split(x_ref[...])

        def solve(right, at):
            width = right.shape[1]
            weights = widen(root_column, width)
            solved = dot_split(x, split(right * weights)) * weights
            high, low = split(solved)
            high_ref[:, at : at + width] = high
            low_ref[:, at : at + width] = low
            return solved

        solve(own[:, :outer], 0)
        solve(other_ref[...], outer)
        interface_ref[...] = -solve(product_ref[...], 2 * outer)
        high, low = split(values_ref[...])
        value_high[...] = high
        value_low[...] = low

    block = rows_ref.shape[0]
    column = column_ref[pl.ds(pl.multiple_of(step * block, block), block), :]
    rows = rows_ref[...] * widen(column, 4 * face) * scale
    across = split(rows[:, outer:])

    def through(at, width):
        cut = slice(at, at + width)
        return dot_split(across, (high_ref[:, cut], low_ref[:, cut]))

    merged_ref[:, :outer] = rows[:, :outer] - through(0, outer)
    merged_ref[:, outer:] = -through(outer, outer)
    local = dot_split(split(rows[:, :outer]), (value_high[...], value_low[...]))
    flux_ref[...] = local - through(2 * outer, flux_ref.shape[1])


def pair_solve(operator, values, scale, schur, other_rows, product):
    nodes = operator.shape[1]
    face = nodes // 4
    outer = 3 * face
    count = values.shape[1]
    width = 2 * outer + count
    whole = lambda shape: pl.BlockSpec(shape, lambda i: (0, 0))
    rows = lambda width: pl.BlockSpec((face, width), lambda i: (i, 0))
    return pl.pallas_call(
        solve_kernel,
        grid=(3,),
        in_specs=[
            rows(nodes),
            pl.BlockSpec((face, nodes), lambda i: (3, 0)),
            whole(values.shape),
            whole(scale.shape),
            whole(schur.shape),
            whole(other_rows.shape),
            whole(product.shape),
        ],
        out_specs=[rows(2 * outer), whole((face, count)), rows(count)],
        out_shape=[
            jax.ShapeDtypeStruct((outer, 2 * outer), F32),
            jax.ShapeDtypeStruct((face, count), F32),
            jax.ShapeDtypeStruct((outer, count), F32),
        ],
        scratch_shapes=[
            pltpu.VMEM((face, width), jnp.bfloat16),
            pltpu.VMEM((face, width), jnp.bfloat16),
            pltpu.VMEM((outer, count), jnp.bfloat16),
            pltpu.VMEM((outer, count), jnp.bfloat16),
            pltpu.VMEM((face, face), F32),
            pltpu.VMEM((face, face), F32),
            pltpu.VMEM((face, face), F32),
            pltpu.VMEM((nodes, 128), F32),
        ],
        compiler_params=pltpu.CompilerParams(vmem_limit_bytes=60 * 2**20),
        name="pair_solve",
    )(operator, operator, values, scale, schur, other_rows, product)


def group_ends(n, expand):
    row = lax.broadcasted_iota(jnp.int32, (n, n), 0)
    col = lax.broadcasted_iota(jnp.int32, (n, n), 1)
    take = (row < n // 2) & (col // 2 == row) if expand else (col < n // 2) & (row == 2 * col)
    return jnp.where(take, 1.0, 0.0).astype(F32)


def exact_dot(a, b):
    return jnp.dot(a, b, precision=HIGHEST, preferred_element_type=F32)


def as_row(x):
    return jnp.concatenate([x[t : t + 1, :] for t in range(x.shape[0])], axis=1)


def triangle(n):
    row = lax.broadcasted_iota(jnp.int32, (n, n), 0)
    col = lax.broadcasted_iota(jnp.int32, (n, n), 1)
    return row, col


def pack_symmetric(block):
    half = block.shape[0] // 2
    row, col = triangle(half)
    first, last = block[:half, :half], block[half:, half:]
    mixed = jnp.where(row >= col, first, last)
    diagonal = jnp.sum(jnp.where(row == col, last, 0.0), axis=0, keepdims=True)
    return block[half:, :half], mixed, diagonal


def unpack_symmetric(corner, mixed, diagonal):
    half = corner.shape[0]
    row, col = triangle(half)
    turned = mixed.T
    first = jnp.where(row >= col, mixed, turned)
    last = jnp.where(row < col, mixed, jnp.where(row == col, diagonal, turned))
    top = jnp.concatenate([first, corner.T], axis=1)
    return jnp.concatenate([top, jnp.concatenate([corner, last], axis=1)], axis=0)


def plan(boxes, samples, face):
    share = face // samples
    across = max(1, boxes * 8 // share)
    columns = 3 * face if across == 1 else 4 * face
    width = columns // across
    height = share * across // boxes
    return share, across, columns, width, height


def exchange_kernel(
    boxes, samples,
    face_ref, values_ref, label_ref, material_ref, permittivity_ref, slot_ref,
    other_ref, schur_ref, total_ref, scale_ref,
    small, small_in, small_staged, small_final, large_in, large_staged, raw, partner,
    send_small, receive_small, send_large, receive_large,
    send_small_2, receive_small_2, send_large_2, receive_large_2,
    send_twin_small, receive_twin_small, send_twin, receive_twin,
):
    me = lax.axis_index("box")
    sample = lax.axis_index("mc")
    face, nodes = face_ref.shape
    outer = 3 * face
    half = face // 2
    share, across, columns, width, height = plan(boxes, samples, face)
    strip = face // boxes
    corner_strip = share // boxes
    at_strip = -(-corner_strip // 8) * 8
    kept = small_staged.shape[1]
    shift = lambda k: lax.rem(me + k + boxes, boxes)
    target = lambda box: {"box": box, "mc": sample}
    MESH = pl.DeviceIdType.MESH

    barrier = pltpu.get_barrier_semaphore()

    def greet(k, carry):
        pl.semaphore_signal(barrier, inc=1, device_id=target(shift(k)), device_id_type=MESH)
        return carry

    lax.fori_loop(1, boxes, greet, 0)
    twins = [lax.rem(sample + t, samples) for t in range(1, samples)]
    for twin in twins:
        pl.semaphore_signal(
            barrier, inc=1, device_id={"box": me, "mc": twin}, device_id_type=MESH
        )

    def offset(i):
        step = (i + 1) // 2
        return boxes // 2 + jnp.where(lax.rem(i, 2) == 0, step, -step)

    def piece(ref, group, j):
        row = group * share + (j // across) * height
        column = lax.rem(j, across) * width
        return ref.at[
            pl.ds(pl.multiple_of(row, 8), height),
            pl.ds(pl.multiple_of(column, 128), width),
        ]

    label = label_ref[...]
    level = jnp.zeros_like(label)
    for w in range(material_ref.shape[0]):
        level = jnp.where(label == w, material_ref[w], level)
    eps = jnp.zeros(label.shape, F32)
    for l in range(permittivity_ref.shape[0]):
        eps = jnp.where(level == l, permittivity_ref[l], eps)
    root = jnp.sqrt(eps)
    scale = as_row(root)
    scale_ref[...] = scale
    column = column_of(scale[:, outer:])
    own = face_ref[:, :outer] * widen(column, outer) * scale[:, :outer]
    product = dot3(own, values_ref[...])
    total_ref[...] = product

    square = face_ref[:, outer:]
    square = 0.5 * (square + square.T)
    corner, mixed, diagonal = pack_symmetric(square)
    mid = root.shape[1] // 2
    row_id = lax.broadcasted_iota(jnp.int32, root.shape, 0)
    lane_id = lax.broadcasted_iota(jnp.int32, root.shape, 1)
    turned = jnp.concatenate([diagonal[:, mid:], diagonal[:, :mid]], axis=1)
    extra = exact_dot(root, group_ends(2 * mid, False))
    extra = jnp.where((lane_id >= mid) & (row_id == 0), turned, extra)
    extra = jnp.where((lane_id >= mid) & (row_id == 1), diagonal, extra)
    packed = jnp.concatenate([corner, mixed], axis=0)
    mine = packed[:share]
    for group in range(1, samples):
        mine = jnp.where(sample == group, packed[group * share : (group + 1) * share], mine)
    for j in range(boxes):
        small[j, :corner_strip, :] = mine[j * corner_strip : (j + 1) * corner_strip, :]
        small[j, at_strip : at_strip + strip, :] = product[j * strip : (j + 1) * strip, :]
    small[:, kept:, :] = jnp.broadcast_to(extra[None], (boxes,) + extra.shape)
    schur_ref[...] = square * widen(column, face) * scale[:, outer:]

    pl.semaphore_wait(barrier, boxes - 1 + samples - 1)

    def send_all(source, landing, send, receive):
        def body(i, carry):
            k = offset(i)
            box = shift(k)
            pltpu.make_async_remote_copy(
                src_ref=source(box), dst_ref=landing, send_sem=send, recv_sem=receive(k),
                device_id=target(box), device_id_type=MESH,
            ).start()
            return carry

        lax.fori_loop(0, boxes - 1, body, 0)

    def drain(buffer, semaphore):
        pltpu.make_async_copy(buffer, buffer, semaphore).wait()

    others = pl.ds(0, boxes - 1)
    send_all(lambda b: small.at[b], small_in.at[me], send_small, lambda k: receive_small)
    send_all(
        lambda b: piece(face_ref, sample, b), large_in.at[me], send_large,
        lambda k: receive_large,
    )
    small_in[me] = small[me]
    large_in[me] = piece(face_ref, sample, me)[...]

    def find(p, carry):
        wanted = slot_ref[p] ^ 1
        partner[p] = lax.fori_loop(
            0, boxes, lambda i, at: jnp.where(slot_ref[i] == wanted, i, at), jnp.int32(0)
        )
        return carry

    lax.fori_loop(0, boxes, find, 0)

    drain(small_in.at[others], receive_small)

    def stage_small(p, carry):
        small_staged[p] = small_in[partner[p], 0:kept, :]
        return carry

    lax.fori_loop(0, boxes, stage_small, 0)
    send_all(
        lambda b: small_staged.at[b], small_final.at[sample, me], send_small_2,
        lambda k: receive_small_2.at[k],
    )
    small_final[sample, me] = small_staged[me]

    drain(large_in.at[others], receive_large)

    def stage_large(p, carry):
        large_staged[p] = large_in[partner[p]]
        return carry

    lax.fori_loop(0, boxes, stage_large, 0)
    send_all(
        lambda b: large_staged.at[b], piece(raw, sample, me), send_large_2,
        lambda k: receive_large_2.at[k],
    )
    piece(raw, sample, me)[...] = large_staged[me]

    def forward(block, send, receive):
        for t, twin in enumerate(twins):
            pltpu.make_async_remote_copy(
                src_ref=block, dst_ref=block, send_sem=send.at[t], recv_sem=receive.at[t],
                device_id={"box": me, "mc": twin}, device_id_type=MESH,
            ).start()

    small_part = lambda group, j: small_final.at[group, j, pl.ds(0, at_strip)]
    forward(small_part(sample, me), send_twin_small, receive_twin_small)

    def pass_small(i, carry):
        k = offset(i)
        source = shift(-k)
        drain(small_final.at[sample, source], receive_small_2.at[k])
        forward(small_part(sample, source), send_twin_small, receive_twin_small)
        return carry

    lax.fori_loop(0, boxes - 1, pass_small, 0)
    forward(piece(raw, sample, me), send_twin, receive_twin)

    def pass_large(i, carry):
        k = offset(i)
        source = shift(-k)
        drain(piece(raw, sample, source), receive_large_2.at[k])
        forward(piece(raw, sample, source), send_twin, receive_twin)
        return carry

    lax.fori_loop(0, boxes - 1, pass_large, 0)

    extra = small_in[partner[me], kept:, :]
    other_scale = as_row(exact_dot(extra, group_ends(2 * mid, True)))
    diagonal = jnp.concatenate([extra[0:1, mid:], extra[1:2, mid:]], axis=1)
    other_column = column_of(other_scale[:, outer:])
    for j in range(boxes):
        total_ref[j * strip : (j + 1) * strip, :] += small_final[
            sample, j, at_strip : at_strip + strip, :
        ]
    for t in range(samples - 1):
        origin = lax.rem(sample + samples - (t + 1), samples)
        drain(small_final.at[origin, :, pl.ds(0, at_strip)], receive_twin_small.at[t])
    pieces = [
        small_final[group, j, :corner_strip, :]
        for group in range(samples) for j in range(boxes)
    ]
    packed = jnp.concatenate(pieces, axis=0)
    square = unpack_symmetric(packed[:half], packed[half:], diagonal)
    schur_ref[...] += square * widen(other_column, face) * other_scale[:, outer:]

    rows_of = lambda ref, group: ref.at[pl.ds(pl.multiple_of(group * share, 8), share)]
    for t in range(samples - 1):
        origin = lax.rem(sample + samples - (t + 1), samples)
        drain(rows_of(raw, origin), receive_twin.at[t])
    other_ref[...] = raw[:, :outer] * widen(other_column, outer) * other_scale[:, :outer]

    drain(small.at[others], send_small)
    drain(large_in.at[others], send_large)
    drain(small_staged.at[others], send_small_2)
    drain(large_staged.at[others], send_large_2)
    for t in range(samples - 1):
        drain(small_final.at[sample, :, pl.ds(0, at_strip)], send_twin_small.at[t])
        drain(rows_of(raw, sample), send_twin.at[t])


def exchange(operator, values, label, material, permittivity, slot):
    boxes = lax.axis_size("box")
    samples = lax.axis_size("mc")
    nodes = operator.shape[1]
    face = nodes // 4
    outer = 3 * face
    count = values.shape[1]
    label = label.reshape(nodes // 128, 128)
    share, across, columns, width, height = plan(boxes, samples, face)
    kept = -(-(share // boxes) // 8) * 8 + -(-(face // boxes) // 8) * 8
    whole = lambda shape: pl.BlockSpec(shape, lambda i: (0, 0))
    scalars = pl.BlockSpec(memory_space=pltpu.SMEM)
    dma = pltpu.SemaphoreType.DMA
    shapes = [(face, outer), (face, face), (face, count), (1, nodes)]
    return pl.pallas_call(
        functools.partial(exchange_kernel, boxes, samples),
        grid=(1,),
        in_specs=[
            pl.BlockSpec((face, nodes), lambda i: (3, 0)),
            whole(values.shape),
            whole(label.shape),
            scalars,
            scalars,
            scalars,
        ],
        out_specs=[whole(shape) for shape in shapes],
        out_shape=[jax.ShapeDtypeStruct(shape, F32) for shape in shapes],
        scratch_shapes=[
            pltpu.VMEM((boxes, kept + nodes // 128, 128), F32),
            pltpu.VMEM((boxes, kept + nodes // 128, 128), F32),
            pltpu.VMEM((boxes, kept, 128), F32),
            pltpu.VMEM((samples, boxes, kept, 128), F32),
            pltpu.VMEM((boxes, height, width), F32),
            pltpu.VMEM((boxes, height, width), F32),
            pltpu.VMEM((face, columns), F32),
            pltpu.SMEM((boxes,), jnp.int32),
            dma, dma, dma, dma,
            dma, dma((boxes,)), dma, dma((boxes,)),
            dma((max(1, samples - 1),)), dma((max(1, samples - 1),)),
            dma((max(1, samples - 1),)), dma((max(1, samples - 1),)),
        ],
        compiler_params=pltpu.CompilerParams(
            collective_id=0, has_side_effects=True, vmem_limit_bytes=60 * 2**20
        ),
        name="exchange",
    )(operator, values, label, material, permittivity, slot)


def per_device(
    base_operator, exterior_values, wire_label, wire_material, permittivity, morton_slot
):
    other_rows, schur, product, scale = exchange(
        base_operator, exterior_values, wire_label, wire_material, permittivity, morton_slot
    )
    return tuple(
        pair_solve(base_operator, exterior_values, scale, schur, other_rows, product)
    )


def solution(mesh):
    return jax.shard_map(
        per_device,
        mesh=mesh,
        in_specs=(P("box", None), P("box", None), P("box", None), P(), P("mc"), P()),
        out_specs=(P(("mc", "box"), None), P(("mc", "box"), None), P(("mc", "box"), None)),
        check_vma=False,
    )
```

time: 61.8 us -> 55.5 us (0.90)
  the two profiles are of different devices: /device:TPU:24 before, /device:TPU:0 now
where the time goes in v2:
time: 55.5 us; the launch traced here: 55.3 us
  Pallas kernels  54.7 us (99%)
  between operations  0.64 us (1%)
    pallas_call x1, Pallas kernels, exchange(): pl.pallas_call(functools.partial(exchange_kernel, boxes, samples), grid=(...  43.8 us
    pallas_call x1, Pallas kernels, pair_solve(): pl.pallas_call(solve_kernel, grid=(3,), in_specs=[rows(nodes), pl.BlockSp...  10.9 us

profile of v2, /device:TPU:0, one launch (start us, length us, event | category | flops | bytes accessed | tf_op | source)
XLA Modules:
  0.0 55.3 jit_solution(14414590589527044514)
XLA Ops:
  0.6 43.8 %exchange.1 = (f32[256,768]{1,0:T(8,128)}, f32[256,256]{1,0:T(8,128)}, f32[256,128]{1,0:T(8,128)}, f32[1,1024]{1,0:T(1,128)}) custom-call(f32[1024,1024]{1,0:T(8,128)} %face_ref.3, f32[768,128]{1,0:T(8,128)} %values_ref.3, s32[8,128]{1,0:T(8,128)} %bitcast.1, s32[64]{0:T(128)} %material_ref.1, f32[8]{0:T(128)} %permittivity_ref.1, s32[16]{0:T(128)} %slot_ref.1), custom_call_target="tpu_custom_call" | custom-call | tf_op jit(solution)/shard_map/exchange/pallas_call | solution.py:480
  44.4 10.9 %pair_solve.1 = (f32[768,1536]{1,0:T(8,128)}, f32[256,128]{1,0:T(8,128)}, f32[768,128]{1,0:T(8,128)}) custom-call(f32[1024,1024]{1,0:T(8,128)} %face_ref.3, f32[1024,1024]{1,0:T(8,128)} %face_ref.3, f32[768,128]{1,0:T(8,128)} %values_ref.3, f32[1,1024]{1,0:T(1,128)} %get-tuple-element.7.scale_ref, f32[256,256]{1,0:T(8,128)} %get-tuple-element.8.schur_ref, ...), custom_call_target="tpu_custom_call" | custom-call | tf_op jit(solution)/shard_map/pair_solve/pallas_call | solution.py:177

commit v3 on v2

--- a/solution.py
+++ b/solution.py
@@ -113,98 +113,146 @@
         direct_inverse(s_ref, x_ref)
 
 
-def solve_kernel(
-    rows_ref, face_ref, values_ref, scale_ref, schur_ref, other_ref, product_ref,
+def fixed_inverse(s):
+    n = s.shape[0]
+    unit = eye(n)
+    alpha = n / jnp.sum(s * s)
+    first = unit - alpha * s
+    parts = split(s)
+    x = alpha * (unit + first)
+    residual = dot3(first, first)
+    yield None
+    x = x + dot3(x, residual)
+    yield None
+    residual = unit - dot_split(parts, split(x))
+    yield None
+    x = x + dot3(x, residual)
+    yield None
+    residual = unit - exact_dot(s, x)
+    yield None
+    yield x + dot3(x, residual), norm(residual)
+
+
+def finish_kernel(
+    left_ref, through_ref, other_ref, interface_in, flux_in, residual_ref,
+    operator_ref, values_ref, scale_ref, schur_ref, product_ref,
     merged_ref, interface_ref, flux_ref,
-    high_ref, low_ref, value_high, value_low, s_ref, x_ref, r_ref, column_ref,
+    other_high, other_low, solved_high, solved_low, rows, s_ref, x_ref, r_ref, column_ref,
+    values, schur, product, semaphore,
 ):
-    face = face_ref.shape[0]
-    outer = 3 * face
+    block = left_ref.shape[0]
+    face, outer = other_ref.shape
     step = pl.program_id(0)
-    scale = scale_ref[...]
-
-    @pl.when(step == 0)
+    fast = residual_ref[0, 0] < 1e-3
+
+    @pl.when(fast)
     def _():
-        column_ref[...] = column_of(scale)
-        own = face_ref[...] * widen(column_ref[outer:, :], 4 * face) * scale
-        s = schur_ref[...]
-        diagonal = jnp.sum(s * eye(face), axis=0, keepdims=True)
-        inverse_root = lax.rsqrt(diagonal)
-        root_column = column_of(inverse_root)
-        s_ref[...] = s * inverse_root * widen(root_column, face)
-        invert(s_ref, x_ref, r_ref)
-        x = split(x_ref[...])
-
-        def solve(right, at):
-            width = right.shape[1]
-            weights = widen(root_column, width)
-            solved = dot_split(x, split(right * weights)) * weights
-            high, low = split(solved)
-            high_ref[:, at : at + width] = high
-            low_ref[:, at : at + width] = low
-            return solved
-
-        solve(own[:, :outer], 0)
-        solve(other_ref[...], outer)
-        interface_ref[...] = -solve(product_ref[...], 2 * outer)
-        high, low = split(values_ref[...])
-        value_high[...] = high
-        value_low[...] = low
-
-    block = rows_ref.shape[0]
-    column = column_ref[pl.ds(pl.multiple_of(step * block, block), block), :]
-    rows = rows_ref[...] * widen(column, 4 * face) * scale
-    across = split(rows[:, outer:])
-
-    def through(at, width):
-        cut = slice(at, at + width)
-        return dot_split(across, (high_ref[:, cut], low_ref[:, cut]))
-
-    merged_ref[:, :outer] = rows[:, :outer] - through(0, outer)
-    merged_ref[:, outer:] = -through(outer, outer)
-    local = dot_split(split(rows[:, :outer]), (value_high[...], value_low[...]))
-    flux_ref[...] = local - through(2 * outer, flux_ref.shape[1])
-
-
-def pair_solve(operator, values, scale, schur, other_rows, product):
-    nodes = operator.shape[1]
-    face = nodes // 4
-    outer = 3 * face
+        @pl.when(step == 0)
+        def _():
+            high, low = split(other_ref[...])
+            other_high[...] = high
+            other_low[...] = low
+            interface_ref[...] = interface_in[...]
+
+        merged_ref[:, :outer] = left_ref[...]
+        through = split(through_ref[...])
+        merged_ref[:, outer:] = -dot_split(through, (other_high[...], other_low[...]))
+        flux_ref[...] = flux_in[...]
+
+    def fetch(source, target):
+        copy = pltpu.make_async_copy(source, target, semaphore)
+        copy.start()
+        copy.wait()
+
+    @pl.when(jnp.logical_not(fast))
+    def _():
+        scale = scale_ref[...]
+
+        @pl.when(step == 0)
+        def _():
+            column_ref[...] = column_of(scale)
+            fetch(operator_ref.at[pl.ds(outer, face)], rows)
+            fetch(values_ref, values)
+            fetch(schur_ref, schur)
+            fetch(product_ref, product)
+            own = rows[:, :outer] * widen(column_ref[outer:, :], outer) * scale[:, :outer]
+            s = schur[...]
+            inverse_root = lax.rsqrt(jnp.sum(s * eye(face), axis=0, keepdims=True))
+            root_column = column_of(inverse_root)
+            s_ref[...] = s * inverse_root * widen(root_column, face)
+            invert(s_ref, x_ref, r_ref)
+            x = split(x_ref[...])
+
+            def solve(right, at):
+                width = right.shape[1]
+                weights = widen(root_column, width)
+                solved = dot_split(x, split(right * weights)) * weights
+                high, low = split(solved)
+                solved_high[:, at : at + width] = high
+                solved_low[:, at : at + width] = low
+                return solved
+
+            solve(own, 0)
+            solve(other_ref[...], outer)
+            interface_ref[...] = -solve(product[...], 2 * outer)
+
+        at = pl.multiple_of(step * block, block)
+        fetch(operator_ref.at[pl.ds(at, block)], rows)
+        mine = rows[...] * widen(column_ref[pl.ds(at, block), :], 4 * face) * scale
+        across = split(mine[:, outer:])
+
+        def apply(at, width):
+            cut = slice(at, at + width)
+            return dot_split(across, (solved_high[:, cut], solved_low[:, cut]))
+
+        merged_ref[:, :outer] = mine[:, :outer] - apply(0, outer)
+        merged_ref[:, outer:] = -apply(outer, outer)
+        local = dot3(mine[:, :outer], values[...])
+        flux_ref[...] = local - apply(2 * outer, flux_ref.shape[1])
+
+
+def finish(left, through, other, interface, flux, residual, operator, values, scale, schur, product):
+    outer = left.shape[0]
+    face = outer // 3
+    nodes = 4 * face
     count = values.shape[1]
     width = 2 * outer + count
-    whole = lambda shape: pl.BlockSpec(shape, lambda i: (0, 0))
+    whole = lambda x: pl.BlockSpec(x.shape, lambda i: (0, 0))
     rows = lambda width: pl.BlockSpec((face, width), lambda i: (i, 0))
+    anywhere = pl.BlockSpec(memory_space=pl.ANY)
+    half = jnp.bfloat16
     return pl.pallas_call(
-        solve_kernel,
+        finish_kernel,
         grid=(3,),
         in_specs=[
-            rows(nodes),
-            pl.BlockSpec((face, nodes), lambda i: (3, 0)),
-            whole(values.shape),
-            whole(scale.shape),
-            whole(schur.shape),
-            whole(other_rows.shape),
-            whole(product.shape),
+            rows(outer), rows(face), whole(other), whole(interface), rows(count),
+            pl.BlockSpec(memory_space=pltpu.SMEM),
+            anywhere, anywhere, whole(scale), anywhere, anywhere,
         ],
-        out_specs=[rows(2 * outer), whole((face, count)), rows(count)],
+        out_specs=[rows(2 * outer), whole(interface), rows(count)],
         out_shape=[
             jax.ShapeDtypeStruct((outer, 2 * outer), F32),
             jax.ShapeDtypeStruct((face, count), F32),
             jax.ShapeDtypeStruct((outer, count), F32),
         ],
         scratch_shapes=[
-            pltpu.VMEM((face, width), jnp.bfloat16),
-            pltpu.VMEM((face, width), jnp.bfloat16),
-            pltpu.VMEM((outer, count), jnp.bfloat16),
-            pltpu.VMEM((outer, count), jnp.bfloat16),
+            pltpu.VMEM((face, outer), half),
+            pltpu.VMEM((face, outer), half),
+            pltpu.VMEM((face, width), half),
+            pltpu.VMEM((face, width), half),
+            pltpu.VMEM((face, nodes), F32),
             pltpu.VMEM((face, face), F32),
             pltpu.VMEM((face, face), F32),
             pltpu.VMEM((face, face), F32),
             pltpu.VMEM((nodes, 128), F32),
+            pltpu.VMEM((outer, count), F32),
+            pltpu.VMEM((face, face), F32),
+            pltpu.VMEM((face, count), F32),
+            pltpu.SemaphoreType.DMA,
         ],
         compiler_params=pltpu.CompilerParams(vmem_limit_bytes=60 * 2**20),
-        name="pair_solve",
-    )(operator, operator, values, scale, schur, other_rows, product)
+        name="finish",
+    )(left, through, other, interface, flux, residual, operator, values, scale, schur, product)
 
 
 def group_ends(n, expand):
@@ -259,8 +307,10 @@
 def exchange_kernel(
     boxes, samples,
     face_ref, values_ref, label_ref, material_ref, permittivity_ref, slot_ref,
-    other_ref, schur_ref, total_ref, scale_ref,
-    small, small_in, small_staged, small_final, large_in, large_staged, raw, partner,
+    operator_ref,
+    left_ref, through_ref, other_ref, interface_ref, flux_ref, residual_ref,
+    scale_ref, schur_ref, total_ref,
+    rest, load, small, small_in, small_staged, small_final, large_in, large_staged, raw, partner,
     send_small, receive_small, send_large, receive_large,
     send_small_2, receive_small_2, send_large_2, receive_large_2,
     send_twin_small, receive_twin_small, send_twin, receive_twin,
@@ -279,6 +329,8 @@
     target = lambda box: {"box": box, "mc": sample}
     MESH = pl.DeviceIdType.MESH
 
+    rest_copy = pltpu.make_async_copy(operator_ref.at[pl.ds(0, outer)], rest, load)
+    rest_copy.start()
     barrier = pltpu.get_barrier_semaphore()
 
     def greet(k, carry):
@@ -316,7 +368,8 @@
     scale_ref[...] = scale
     column = column_of(scale[:, outer:])
     own = face_ref[:, :outer] * widen(column, outer) * scale[:, :outer]
-    product = dot3(own, values_ref[...])
+    own_parts = split(own)
+    product = dot_split(own_parts, split(values_ref[...]))
     total_ref[...] = product
 
     square = face_ref[:, outer:]
@@ -374,6 +427,13 @@
 
     lax.fori_loop(0, boxes, find, 0)
 
+    rest_copy.wait()
+    values_parts = split(values_ref[...])
+    for at in range(0, outer, face):
+        cut = slice(at, at + face)
+        rest[cut, :] = rest[cut, :] * widen(column_of(scale[:, cut]), nodes) * scale
+        flux_ref[cut, :] = dot_split(split(rest[cut, :outer]), values_parts)
+
     drain(small_in.at[others], receive_small)
 
     def stage_small(p, carry):
@@ -418,17 +478,6 @@
         return carry
 
     lax.fori_loop(0, boxes - 1, pass_small, 0)
-    forward(piece(raw, sample, me), send_twin, receive_twin)
-
-    def pass_large(i, carry):
-        k = offset(i)
-        source = shift(-k)
-        drain(piece(raw, sample, source), receive_large_2.at[k])
-        forward(piece(raw, sample, source), send_twin, receive_twin)
-        return carry
-
-    lax.fori_loop(0, boxes - 1, pass_large, 0)
-
     extra = small_in[partner[me], kept:, :]
     other_scale = as_row(exact_dot(extra, group_ends(2 * mid, True)))
     diagonal = jnp.concatenate([extra[0:1, mid:], extra[1:2, mid:]], axis=1)
@@ -448,6 +497,46 @@
     square = unpack_symmetric(packed[:half], packed[half:], diagonal)
     schur_ref[...] += square * widen(other_column, face) * other_scale[:, outer:]
 
+    forward(piece(raw, sample, me), send_twin, receive_twin)
+
+    def pass_large(i, carry):
+        k = offset(i)
+        source = shift(-k)
+        drain(piece(raw, sample, source), receive_large_2.at[k])
+        forward(piece(raw, sample, source), send_twin, receive_twin)
+        return carry
+
+    def work():
+        schur = schur_ref[...]
+        inverse_root = lax.rsqrt(jnp.sum(schur * eye(face), axis=0, keepdims=True))
+        weights = widen(column_of(inverse_root), face) * inverse_root
+        for result in fixed_inverse(schur * weights):
+            if result is None:
+                yield
+        x, size = result
+        residual_ref[0, 0] = size
+        inverse = split(x * weights)
+        total = split(total_ref[...])
+        interface_ref[...] = -dot_split(inverse, total)
+        yield
+        for at in range(0, outer, face):
+            cut = slice(at, at + face)
+            through = dot_split(split(rest[cut, outer:]), inverse)
+            through_ref[cut, :] = through
+            through = split(through)
+            flux_ref[cut, :] -= dot_split(through, total)
+            yield
+            left_ref[cut, :] = rest[cut, :outer] - dot_split(through, own_parts)
+            yield
+
+    parts = 12
+    done = 0
+    for part, _ in enumerate(work()):
+        upto = min(boxes - 1, (part + 1) * (boxes - 1) // parts)
+        lax.fori_loop(done, upto, pass_large, 0)
+        done = upto
+    lax.fori_loop(done, boxes - 1, pass_large, 0)
+
     rows_of = lambda ref, group: ref.at[pl.ds(pl.multiple_of(group * share, 8), share)]
     for t in range(samples - 1):
         origin = lax.rem(sample + samples - (t + 1), samples)
@@ -476,7 +565,10 @@
     whole = lambda shape: pl.BlockSpec(shape, lambda i: (0, 0))
     scalars = pl.BlockSpec(memory_space=pltpu.SMEM)
     dma = pltpu.SemaphoreType.DMA
-    shapes = [(face, outer), (face, face), (face, count), (1, nodes)]
+    shapes = [
+        (outer, outer), (outer, face), (face, outer), (face, count), (outer, count), (1, 1),
+        (1, nodes), (face, face), (face, count),
+    ]
     return pl.pallas_call(
         functools.partial(exchange_kernel, boxes, samples),
         grid=(1,),
@@ -487,10 +579,13 @@
             scalars,
             scalars,
             scalars,
+            pl.BlockSpec(memory_space=pl.ANY),
         ],
-        out_specs=[whole(shape) for shape in shapes],
+        out_specs=[scalars if shape == (1, 1) else whole(shape) for shape in shapes],
         out_shape=[jax.ShapeDtypeStruct(shape, F32) for shape in shapes],
         scratch_shapes=[
+            pltpu.VMEM((outer, nodes), F32),
+            dma,
             pltpu.VMEM((boxes, kept + nodes // 128, 128), F32),
             pltpu.VMEM((boxes, kept + nodes // 128, 128), F32),
             pltpu.VMEM((boxes, kept, 128), F32),
@@ -508,17 +603,21 @@
             collective_id=0, has_side_effects=True, vmem_limit_bytes=60 * 2**20
         ),
         name="exchange",
-    )(operator, values, label, material, permittivity, slot)
+    )(operator, values, label, material, permittivity, slot, operator)
 
 
 def per_device(
     base_operator, exterior_values, wire_label, wire_material, permittivity, morton_slot
 ):
-    other_rows, schur, product, scale = exchange(
+    parts = exchange(
         base_operator, exterior_values, wire_label, wire_material, permittivity, morton_slot
     )
+    left, through, other, interface, flux, residual, scale, schur, product = parts
     return tuple(
-        pair_solve(base_operator, exterior_values, scale, schur, other_rows, product)
+        finish(
+            left, through, other, interface, flux, residual,
+            base_operator, exterior_values, scale, schur, product,
+        )
     )
 
 

time: 55.5 us -> 52.9 us (0.953)
  Pallas kernels: 54.7 us -> 52 us
    pallas_call x1, Pallas kernels: 10.9 us -> 6.75 us  [finish(): pl.pallas_call(finish_kernel, grid=(3,), in_specs=[rows(outer), rows(face...]
    pallas_call x1, Pallas kernels: 43.8 us -> 45.3 us  [exchange(): pl.pallas_call(functools.partial(exchange_kernel, boxes, samples), grid=(...]
where the time goes in v3:
time: 52.9 us; the launch traced here: 52.7 us
  Pallas kernels  52 us (98%)
  between operations  0.64 us (1%)
    pallas_call x1, Pallas kernels, exchange(): pl.pallas_call(functools.partial(exchange_kernel, boxes, samples), grid=(...  45.3 us
    pallas_call x1, Pallas kernels, finish(): pl.pallas_call(finish_kernel, grid=(3,), in_specs=[rows(outer), rows(face...  6.75 us

profile of v3, /device:TPU:0, one launch (start us, length us, event | category | flops | bytes accessed | tf_op | source)
XLA Modules:
  0.0 52.7 jit_solution(10991067432582491607)
XLA Ops:
  0.6 45.3 %exchange.1 = (f32[768,768]{1,0:T(8,128)}, f32[768,256]{1,0:T(8,128)}, f32[256,768]{1,0:T(8,128)}, f32[256,128]{1,0:T(8,128)}, f32[768,128]{1,0:T(8,128)}, /*ind...) custom-call(f32[1024,1024]{1,0:T(8,128)} %operator_ref.3, f32[768,128]{1,0:T(8,128)} %values_ref.3, ...), custom_call_target="tpu_custom_call" | custom-call | tf_op jit(solution)/shard_map/exchange/pallas_call | solution.py:572
  45.9 6.8 %finish.1 = (f32[768,1536]{1,0:T(8,128)}, f32[256,128]{1,0:T(8,128)}, f32[768,128]{1,0:T(8,128)}) custom-call(f32[768,768]{1,0:T(8,128)} %get-tuple-element.12.left_ref, f32[768,256]{1,0:T(8,128)} %get-tuple-element.13.through_ref, f32[256,768]{1,0:T(8,128)} %get-tuple-element.14.other_ref, f32[256,128]{1,0:T(8,128)} %get-tuple-element.15.interface_in, ...), custom_call_target="tpu_custom_call" | custom-call | tf_op jit(solution)/shard_map/finish/pallas_call | solution.py:224

commit v4 on v3

--- a/solution.py
+++ b/solution.py
@@ -306,10 +306,11 @@
 
 def exchange_kernel(
     boxes, samples,
-    face_ref, values_ref, label_ref, material_ref, permittivity_ref, slot_ref,
-    operator_ref,
-    left_ref, through_ref, other_ref, interface_ref, flux_ref, residual_ref,
-    scale_ref, schur_ref, total_ref,
+    operator_hbm, values_hbm, label_hbm, material_ref, permittivity_ref, slot_ref,
+    left_hbm, through_hbm, other_hbm, interface_hbm, flux_hbm, scale_hbm, schur_hbm,
+    total_hbm, residual_ref,
+    left_ref, through_ref, other_ref, interface_ref, flux_ref, scale_ref, schur_ref,
+    total_ref, stored, face_ref, values_ref, label_ref, loaded,
     rest, load, small, small_in, small_staged, small_final, large_in, large_staged, raw, partner,
     send_small, receive_small, send_large, receive_large,
     send_small_2, receive_small_2, send_large_2, receive_large_2,
@@ -320,6 +321,18 @@
     face, nodes = face_ref.shape
     outer = 3 * face
     half = face // 2
+    results = [
+        (left_ref, left_hbm), (through_ref, through_hbm), (other_ref, other_hbm),
+        (interface_ref, interface_hbm), (flux_ref, flux_hbm), (scale_ref, scale_hbm),
+        (schur_ref, schur_hbm), (total_ref, total_hbm),
+    ]
+
+    def store(index, cut=None):
+        source, target = results[index]
+        if cut is not None:
+            source, target = source.at[cut], target.at[cut]
+        pltpu.make_async_copy(source, target, stored.at[index]).start()
+
     share, across, columns, width, height = plan(boxes, samples, face)
     strip = face // boxes
     corner_strip = share // boxes
@@ -329,7 +342,14 @@
     target = lambda box: {"box": box, "mc": sample}
     MESH = pl.DeviceIdType.MESH
 
-    rest_copy = pltpu.make_async_copy(operator_ref.at[pl.ds(0, outer)], rest, load)
+    loads = [
+        pltpu.make_async_copy(operator_hbm.at[pl.ds(outer, face)], face_ref, loaded.at[0]),
+        pltpu.make_async_copy(label_hbm, label_ref, loaded.at[1]),
+        pltpu.make_async_copy(values_hbm, values_ref, loaded.at[2]),
+    ]
+    for copy in loads:
+        copy.start()
+    rest_copy = pltpu.make_async_copy(operator_hbm.at[pl.ds(0, outer)], rest, load)
     rest_copy.start()
     barrier = pltpu.get_barrier_semaphore()
 
@@ -348,13 +368,46 @@
         step = (i + 1) // 2
         return boxes // 2 + jnp.where(lax.rem(i, 2) == 0, step, -step)
 
-    def piece(ref, group, j):
+    halves = len(large_in)
+    narrow = width // halves
+
+    def piece(ref, group, j, part):
         row = group * share + (j // across) * height
-        column = lax.rem(j, across) * width
+        column = lax.rem(j, across) * width + part * narrow
         return ref.at[
             pl.ds(pl.multiple_of(row, 8), height),
-            pl.ds(pl.multiple_of(column, 128), width),
+            pl.ds(pl.multiple_of(column, 128), narrow),
         ]
+
+    def send_all(source, landing, send, receive):
+        def body(i, carry):
+            k = offset(i)
+            box = shift(k)
+            pltpu.make_async_remote_copy(
+                src_ref=source(box), dst_ref=landing, send_sem=send, recv_sem=receive(k),
+                device_id=target(box), device_id_type=MESH,
+            ).start()
+            return carry
+
+        lax.fori_loop(0, boxes - 1, body, 0)
+
+    def drain(buffer, semaphore):
+        pltpu.make_async_copy(buffer, buffer, semaphore).wait()
+
+    others = pl.ds(0, boxes - 1)
+
+    def send_part(part):
+        send_all(
+            lambda b: piece(face_ref, sample, b, part), large_in[part].at[me],
+            send_large.at[part], lambda k: receive_large.at[part],
+        )
+        large_in[part][me] = piece(face_ref, sample, me, part)[...]
+
+    loads[0].wait()
+    pl.semaphore_wait(barrier, boxes - 1 + samples - 1)
+    send_part(0)
+    loads[1].wait()
+    loads[2].wait()
 
     label = label_ref[...]
     level = jnp.zeros_like(label)
@@ -392,31 +445,11 @@
     small[:, kept:, :] = jnp.broadcast_to(extra[None], (boxes,) + extra.shape)
     schur_ref[...] = square * widen(column, face) * scale[:, outer:]
 
-    pl.semaphore_wait(barrier, boxes - 1 + samples - 1)
-
-    def send_all(source, landing, send, receive):
-        def body(i, carry):
-            k = offset(i)
-            box = shift(k)
-            pltpu.make_async_remote_copy(
-                src_ref=source(box), dst_ref=landing, send_sem=send, recv_sem=receive(k),
-                device_id=target(box), device_id_type=MESH,
-            ).start()
-            return carry
-
-        lax.fori_loop(0, boxes - 1, body, 0)
-
-    def drain(buffer, semaphore):
-        pltpu.make_async_copy(buffer, buffer, semaphore).wait()
-
-    others = pl.ds(0, boxes - 1)
     send_all(lambda b: small.at[b], small_in.at[me], send_small, lambda k: receive_small)
-    send_all(
-        lambda b: piece(face_ref, sample, b), large_in.at[me], send_large,
-        lambda k: receive_large,
-    )
     small_in[me] = small[me]
-    large_in[me] = piece(face_ref, sample, me)[...]
+    for part in range(1, halves):
+        send_part(part)
+    store(5)
 
     def find(p, carry):
         wanted = slot_ref[p] ^ 1
@@ -447,18 +480,19 @@
     )
     small_final[sample, me] = small_staged[me]
 
-    drain(large_in.at[others], receive_large)
-
-    def stage_large(p, carry):
-        large_staged[p] = large_in[partner[p]]
-        return carry
-
-    lax.fori_loop(0, boxes, stage_large, 0)
-    send_all(
-        lambda b: large_staged.at[b], piece(raw, sample, me), send_large_2,
-        lambda k: receive_large_2.at[k],
-    )
-    piece(raw, sample, me)[...] = large_staged[me]
+    for part in range(halves):
+        drain(large_in[part].at[others], receive_large.at[part])
+
+        def stage_large(p, carry):
+            large_staged[part, p] = large_in[part][partner[p]]
+            return carry
+
+        lax.fori_loop(0, boxes, stage_large, 0)
+        send_all(
+            lambda b: large_staged.at[part, b], piece(raw, sample, me, part),
+            send_large_2.at[part], lambda k: receive_large_2.at[part, k],
+        )
+        piece(raw, sample, me, part)[...] = large_staged[part, me]
 
     def forward(block, send, receive):
         for t, twin in enumerate(twins):
@@ -497,16 +531,22 @@
     square = unpack_symmetric(packed[:half], packed[half:], diagonal)
     schur_ref[...] += square * widen(other_column, face) * other_scale[:, outer:]
 
-    forward(piece(raw, sample, me), send_twin, receive_twin)
-
-    def pass_large(i, carry):
-        k = offset(i)
-        source = shift(-k)
-        drain(piece(raw, sample, source), receive_large_2.at[k])
-        forward(piece(raw, sample, source), send_twin, receive_twin)
-        return carry
+    for part in range(halves):
+        forward(piece(raw, sample, me, part), send_twin, receive_twin)
+
+    def pass_large(part):
+        def body(i, carry):
+            k = offset(i)
+            source = shift(-k)
+            drain(piece(raw, sample, source, part), receive_large_2.at[part, k])
+            forward(piece(raw, sample, source, part), send_twin, receive_twin)
+            return carry
+
+        return body
 
     def work():
+        store(6)
+        store(7)
         schur = schur_ref[...]
         inverse_root = lax.rsqrt(jnp.sum(schur * eye(face), axis=0, keepdims=True))
         weights = widen(column_of(inverse_root), face) * inverse_root
@@ -518,6 +558,7 @@
         inverse = split(x * weights)
         total = split(total_ref[...])
         interface_ref[...] = -dot_split(inverse, total)
+        store(3)
         yield
         for at in range(0, outer, face):
             cut = slice(at, at + face)
@@ -525,31 +566,46 @@
             through_ref[cut, :] = through
             through = split(through)
             flux_ref[cut, :] -= dot_split(through, total)
+            store(1, cut)
+            store(4, cut)
             yield
             left_ref[cut, :] = rest[cut, :outer] - dot_split(through, own_parts)
+            store(0, cut)
             yield
 
     parts = 12
+    steps = [(part, i) for part in range(halves) for i in range(boxes - 1)]
+
+    def pass_steps(first, last):
+        for part in range(halves):
+            mine = [i for p, i in steps[first:last] if p == part]
+            if mine:
+                lax.fori_loop(mine[0], mine[-1] + 1, pass_large(part), 0)
+
     done = 0
-    for part, _ in enumerate(work()):
-        upto = min(boxes - 1, (part + 1) * (boxes - 1) // parts)
-        lax.fori_loop(done, upto, pass_large, 0)
+    for count, _ in enumerate(work()):
+        upto = min(len(steps), (count + 1) * len(steps) // parts)
+        pass_steps(done, upto)
         done = upto
-    lax.fori_loop(done, boxes - 1, pass_large, 0)
+    pass_steps(done, len(steps))
 
     rows_of = lambda ref, group: ref.at[pl.ds(pl.multiple_of(group * share, 8), share)]
     for t in range(samples - 1):
         origin = lax.rem(sample + samples - (t + 1), samples)
         drain(rows_of(raw, origin), receive_twin.at[t])
     other_ref[...] = raw[:, :outer] * widen(other_column, outer) * other_scale[:, :outer]
+    store(2)
 
     drain(small.at[others], send_small)
-    drain(large_in.at[others], send_large)
+    for part in range(halves):
+        drain(large_in[part].at[others], send_large.at[part])
+        drain(large_staged.at[part, others], send_large_2.at[part])
     drain(small_staged.at[others], send_small_2)
-    drain(large_staged.at[others], send_large_2)
     for t in range(samples - 1):
         drain(small_final.at[sample, :, pl.ds(0, at_strip)], send_twin_small.at[t])
         drain(rows_of(raw, sample), send_twin.at[t])
+    for index, (source, target) in enumerate(results):
+        pltpu.make_async_copy(source, target, stored.at[index]).wait()
 
 
 def exchange(operator, values, label, material, permittivity, slot):
@@ -562,40 +618,37 @@
     label = label.reshape(nodes // 128, 128)
     share, across, columns, width, height = plan(boxes, samples, face)
     kept = -(-(share // boxes) // 8) * 8 + -(-(face // boxes) // 8) * 8
-    whole = lambda shape: pl.BlockSpec(shape, lambda i: (0, 0))
+    halves = 2 if width % 256 == 0 else (3 if width % 384 == 0 else 1)
+    held = pl.BlockSpec(memory_space=pltpu.HBM)
     scalars = pl.BlockSpec(memory_space=pltpu.SMEM)
     dma = pltpu.SemaphoreType.DMA
     shapes = [
-        (outer, outer), (outer, face), (face, outer), (face, count), (outer, count), (1, 1),
+        (outer, outer), (outer, face), (face, outer), (face, count), (outer, count),
         (1, nodes), (face, face), (face, count),
     ]
     return pl.pallas_call(
         functools.partial(exchange_kernel, boxes, samples),
-        grid=(1,),
-        in_specs=[
-            pl.BlockSpec((face, nodes), lambda i: (3, 0)),
-            whole(values.shape),
-            whole(label.shape),
-            scalars,
-            scalars,
-            scalars,
-            pl.BlockSpec(memory_space=pl.ANY),
-        ],
-        out_specs=[scalars if shape == (1, 1) else whole(shape) for shape in shapes],
-        out_shape=[jax.ShapeDtypeStruct(shape, F32) for shape in shapes],
-        scratch_shapes=[
+        in_specs=[held, held, held, scalars, scalars, scalars],
+        out_specs=[pl.BlockSpec(memory_space=pl.ANY)] * len(shapes) + [scalars],
+        out_shape=[jax.ShapeDtypeStruct(shape, F32) for shape in shapes + [(1, 1)]],
+        scratch_shapes=[pltpu.VMEM(shape, F32) for shape in shapes] + [
+            dma((len(shapes),)),
+            pltpu.VMEM((face, nodes), F32),
+            pltpu.VMEM(values.shape, F32),
+            pltpu.VMEM(label.shape, jnp.int32),
+            dma((3,)),
             pltpu.VMEM((outer, nodes), F32),
             dma,
             pltpu.VMEM((boxes, kept + nodes // 128, 128), F32),
             pltpu.VMEM((boxes, kept + nodes // 128, 128), F32),
             pltpu.VMEM((boxes, kept, 128), F32),
             pltpu.VMEM((samples, boxes, kept, 128), F32),
-            pltpu.VMEM((boxes, height, width), F32),
-            pltpu.VMEM((boxes, height, width), F32),
+            (pltpu.VMEM((boxes, height, width // halves), F32),) * halves,
+            pltpu.VMEM((halves, boxes, height, width // halves), F32),
             pltpu.VMEM((face, columns), F32),
             pltpu.SMEM((boxes,), jnp.int32),
-            dma, dma, dma, dma,
-            dma, dma((boxes,)), dma, dma((boxes,)),
+            dma, dma, dma((halves,)), dma((halves,)),
+            dma, dma((boxes,)), dma((halves,)), dma((halves, boxes)),
             dma((max(1, samples - 1),)), dma((max(1, samples - 1),)),
             dma((max(1, samples - 1),)), dma((max(1, samples - 1),)),
         ],
@@ -603,7 +656,7 @@
             collective_id=0, has_side_effects=True, vmem_limit_bytes=60 * 2**20
         ),
         name="exchange",
-    )(operator, values, label, material, permittivity, slot, operator)
+    )(operator, values, label, material, permittivity, slot)
 
 
 def per_device(
@@ -612,7 +665,7 @@
     parts = exchange(
         base_operator, exterior_values, wire_label, wire_material, permittivity, morton_slot
     )
-    left, through, other, interface, flux, residual, scale, schur, product = parts
+    left, through, other, interface, flux, scale, schur, product, residual = parts
     return tuple(
         finish(
             left, through, other, interface, flux, residual,

time: 52.9 us -> 51.9 us (0.981)
  Pallas kernels: 52 us -> 51 us
    pallas_call x1, Pallas kernels: 45.3 us -> 44.3 us  [exchange(): pl.pallas_call(functools.partial(exchange_kernel, boxes, samples), in_spe...]
where the time goes in v4:
time: 51.9 us; the launch traced here: 51.7 us
  Pallas kernels  51 us (98%)
  between operations  0.64 us (1%)
    pallas_call x1, Pallas kernels, exchange(): pl.pallas_call(functools.partial(exchange_kernel, boxes, samples), in_spe...  44.3 us
    pallas_call x1, Pallas kernels, finish(): pl.pallas_call(finish_kernel, grid=(3,), in_specs=[rows(outer), rows(face...  6.75 us

profile of v4, /device:TPU:0, one launch (start us, length us, event | category | flops | bytes accessed | tf_op | source)
XLA Modules:
  0.0 51.7 jit_solution(15492549754421185762)
XLA Ops:
  0.6 44.3 %exchange.1 = (f32[768,768]{1,0:T(8,128)}, f32[768,256]{1,0:T(8,128)}, f32[256,768]{1,0:T(8,128)}, f32[256,128]{1,0:T(8,128)}, f32[768,128]{1,0:T(8,128)}, /*ind...) custom-call(f32[1024,1024]{1,0:T(8,128)} %operator_ref.1, f32[768,128]{1,0:T(8,128)} %values_ref.1, ...), custom_call_target="tpu_custom_call" | custom-call | tf_op jit(solution)/shard_map/exchange/pallas_call | solution.py:629
  44.9 6.8 %finish.1 = (f32[768,1536]{1,0:T(8,128)}, f32[256,128]{1,0:T(8,128)}, f32[768,128]{1,0:T(8,128)}) custom-call(f32[768,768]{1,0:T(8,128)} %get-tuple-element.12.left_ref, f32[768,256]{1,0:T(8,128)} %get-tuple-element.13.through_ref, f32[256,768]{1,0:T(8,128)} %get-tuple-element.14.other_ref, f32[256,128]{1,0:T(8,128)} %get-tuple-element.15.interface_in, ...), custom_call_target="tpu_custom_call" | custom-call | tf_op jit(solution)/shard_map/finish/pallas_call | solution.py:224

commit v5 on v4

--- a/solution.py
+++ b/solution.py
@@ -447,8 +447,6 @@
 
     send_all(lambda b: small.at[b], small_in.at[me], send_small, lambda k: receive_small)
     small_in[me] = small[me]
-    for part in range(1, halves):
-        send_part(part)
     store(5)
 
     def find(p, carry):
@@ -467,6 +465,9 @@
         rest[cut, :] = rest[cut, :] * widen(column_of(scale[:, cut]), nodes) * scale
         flux_ref[cut, :] = dot_split(split(rest[cut, :outer]), values_parts)
 
+    drain(small.at[others], send_small)
+    for part in range(1, halves):
+        send_part(part)
     drain(small_in.at[others], receive_small)
 
     def stage_small(p, carry):
@@ -479,6 +480,7 @@
         lambda k: receive_small_2.at[k],
     )
     small_final[sample, me] = small_staged[me]
+    drain(small_staged.at[others], send_small_2)
 
     for part in range(halves):
         drain(large_in[part].at[others], receive_large.at[part])
@@ -596,11 +598,9 @@
     other_ref[...] = raw[:, :outer] * widen(other_column, outer) * other_scale[:, :outer]
     store(2)
 
-    drain(small.at[others], send_small)
     for part in range(halves):
         drain(large_in[part].at[others], send_large.at[part])
         drain(large_staged.at[part, others], send_large_2.at[part])
-    drain(small_staged.at[others], send_small_2)
     for t in range(samples - 1):
         drain(small_final.at[sample, :, pl.ds(0, at_strip)], send_twin_small.at[t])
         drain(rows_of(raw, sample), send_twin.at[t])

time: 51.9 us -> 52.4 us (level); the launches traced: 51.7 us -> 51.5 us
  no operation moved by 1% of the time
where the time goes in v5:
time: 52.4 us; the launch traced here: 51.5 us
  Pallas kernels  50.9 us (97%)
  between operations  0.64 us (1%)
    pallas_call x1, Pallas kernels, exchange(): pl.pallas_call(functools.partial(exchange_kernel, boxes, samples), in_spe...  44.1 us
    pallas_call x1, Pallas kernels, finish(): pl.pallas_call(finish_kernel, grid=(3,), in_specs=[rows(outer), rows(face...  6.75 us

profile of v5, /device:TPU:0, one launch (start us, length us, event | category | flops | bytes accessed | tf_op | source)
XLA Modules:
  0.0 51.5 jit_solution(2109235738805750527)
XLA Ops:
  0.6 44.1 %exchange.1 = (f32[768,768]{1,0:T(8,128)}, f32[768,256]{1,0:T(8,128)}, f32[256,768]{1,0:T(8,128)}, f32[256,128]{1,0:T(8,128)}, f32[768,128]{1,0:T(8,128)}, /*ind...) custom-call(f32[1024,1024]{1,0:T(8,128)} %operator_ref.1, f32[768,128]{1,0:T(8,128)} %values_ref.1, ...), custom_call_target="tpu_custom_call" | custom-call | tf_op jit(solution)/shard_map/exchange/pallas_call | solution.py:629
  44.8 6.8 %finish.1 = (f32[768,1536]{1,0:T(8,128)}, f32[256,128]{1,0:T(8,128)}, f32[768,128]{1,0:T(8,128)}) custom-call(f32[768,768]{1,0:T(8,128)} %get-tuple-element.12.left_ref, f32[768,256]{1,0:T(8,128)} %get-tuple-element.13.through_ref, f32[256,768]{1,0:T(8,128)} %get-tuple-element.14.other_ref, f32[256,128]{1,0:T(8,128)} %get-tuple-element.15.interface_in, ...), custom_call_target="tpu_custom_call" | custom-call | tf_op jit(solution)/shard_map/finish/pallas_call | solution.py:224
